TPU v7x, 32 devices: a whole 2x2x4 slice. The times are simulated.
32 devices in a mesh: cp: 16 (over z, x, core), hd: 2 (over y).
Axes of the slice: x: 2, y: 2, z: 4, core: 2. Of those that a mesh axis runs over, the one named last changes fastest.
Arguments:
- query: bfloat16 [8192, 512], P('cp', 'hd'), may hold values from -6 to 6
- keys: bfloat16 [8192, 128], P('cp'), may hold values from -4 to 4
- values: bfloat16 [8192, 128], P('cp'), may hold values from -4 to 6
- grad_out: bfloat16 [8192, 512], P('cp', 'hd'), may hold values from -6 to 6
- doc_start: int32 [8192], P('cp'), may hold values from 0 to 8191, as said below
Outputs:
- grad_query: bfloat16 [8192, 512], P('cp', 'hd')
- grad_keys: bfloat16 [8192, 128], P('cp')
- grad_values: bfloat16 [8192, 128], P('cp')
Inputs may be any that keep to these rules, and one draw needn't show every extreme that they name: `doc_start`: documents are contiguous runs of tokens of at most 4096 tokens; no document crosses a multiple of 4096 tokens; the first 4096 tokens form one document; the last token forms a document of its own.
All inputs are finite; a program needn't handle non-finite values.
Results may differ from a plain program's by a relative error of at most 0.0075.
Values may be sent and summed in bfloat16 or wider, within the bound.
A program may use at most 64 MiB of HBM per device.

v0:
```python
import math

import jax
import jax.numpy as jnp
from jax import lax
from jax.sharding import PartitionSpec as P

HDIM = 128
SPAN = 8


masked_score = -1e30


def passed_along(array, axis, by):
    length = lax.axis_size(axis)
    pairs = [(i, i + by) for i in range(length) if 0 <= i + by < length]
    return lax.ppermute(array, axis, pairs)


def shifted(array, axis, by):
    length = lax.axis_size(axis)
    return lax.ppermute(array, axis, [(i, (i + by) % length) for i in range(length)])


def key_mask(start_rows, query_base, key_base, row_count, key_width):
    query_pos = query_base + lax.iota(jnp.int32, row_count)
    key_pos = key_base + lax.iota(jnp.int32, key_width)
    inside = (key_pos[None, :] >= start_rows[:, None]) & (key_pos[None, :] <= query_pos[:, None])
    return inside & True


def stat_block(
    statistics, query_heads, grad_heads, start_rows, query_base, key_block, value_block, key_base
):
    row_count = query_heads.shape[0]
    key_width = min(512, key_block.shape[0])
    scaling = 1.0 / math.sqrt(query_heads.shape[2])
    running_max, running_sum, weighted = statistics
    allowed = key_mask(start_rows, query_base, key_base + 0, row_count, key_width)
    scores = (
        jnp.einsum("thd,kd->htk", query_heads, key_block, preferred_element_type=jnp.float32)
        * scaling
    )
    scores = jnp.where(allowed[None], scores, masked_score)
    new_max = jnp.maximum(running_max, jnp.max(scores, axis=-1))
    unnormed = jnp.where(allowed[None], jnp.exp(scores - new_max[..., None]), 0.0)
    grad_prob = jnp.einsum(
        "thd,kd->htk", grad_heads, value_block, preferred_element_type=jnp.float32
    )
    factor = jnp.exp(running_max - new_max)
    running_sum = running_sum * factor + jnp.sum(unnormed, axis=-1)
    weighted = weighted * factor + jnp.sum(unnormed * grad_prob, axis=-1)
    return (new_max, running_sum, weighted)


def grad_block(
    query_heads,
    grad_heads,
    log_norm,
    row_delta,
    start_rows,
    query_base,
    key_block,
    value_block,
    key_base,
):
    row_count = query_heads.shape[0]
    key_width = min(512, key_block.shape[0])
    scaling = 1.0 / math.sqrt(query_heads.shape[2])
    allowed = key_mask(start_rows, query_base, key_base + 0, row_count, key_width)
    scores = (
        jnp.einsum("thd,kd->htk", query_heads, key_block, preferred_element_type=jnp.float32)
        * scaling
    )
    probs = jnp.where(allowed[None], jnp.exp(scores - log_norm[..., None]), 0.0)
    grad_prob = jnp.einsum(
        "thd,kd->htk", grad_heads, value_block, preferred_element_type=jnp.float32
    )
    grad_score = (probs * (grad_prob - row_delta[..., None])).astype(jnp.bfloat16)
    probs_low = probs.astype(jnp.bfloat16)
    grad_query = jnp.einsum(
        "htk,kd->thd", grad_score, key_block, preferred_element_type=jnp.float32
    )
    key_terms = jnp.einsum(
        "htk,thd->kd", grad_score, query_heads, preferred_element_type=jnp.float32
    )
    value_terms = jnp.einsum(
        "htk,thd->kd", probs_low, grad_heads, preferred_element_type=jnp.float32
    )
    return (grad_query, key_terms, value_terms)


def body(query, keys, values, grad_out, doc_start):
    row_count = query.shape[0]
    head_count = query.shape[1] // HDIM
    scaling = 1.0 / math.sqrt(HDIM)
    position = lax.axis_index("cp")
    query_heads = query.reshape(row_count, head_count, HDIM)
    grad_heads = grad_out.reshape(row_count, head_count, HDIM)
    own_base = position * row_count
    row_zeros = jnp.zeros((head_count, row_count), jnp.float32)
    statistics = (
        jnp.full((head_count, row_count), masked_score, jnp.float32),
        row_zeros,
        row_zeros,
    )
    key_acc = jnp.zeros((row_count, HDIM), jnp.float32)
    value_acc = jnp.zeros((row_count, HDIM), jnp.float32)
    key_cur, value_cur = (keys, values)
    held_blocks = []
    for offset in range(SPAN):
        held_blocks.append((key_cur, value_cur))
        statistics = stat_block(
            statistics,
            query_heads,
            grad_heads,
            doc_start,
            own_base,
            key_cur,
            value_cur,
            (position - offset) * row_count,
        )
        if offset + 1 < SPAN:
            key_cur, value_cur = passed_along((key_cur, value_cur), "cp", 1)
    running_max, running_sum, weighted = statistics
    log_norm = running_max + jnp.log(running_sum)
    row_delta = weighted / running_sum
    grad_query = jnp.zeros((row_count, head_count, HDIM), jnp.float32)
    key_cur, value_cur = (keys, values)
    for offset in range(SPAN):
        part_query, part_key, part_value = grad_block(
            query_heads,
            grad_heads,
            log_norm,
            row_delta,
            doc_start,
            own_base,
            key_cur,
            value_cur,
            (position - offset) * row_count,
        )
        grad_query = grad_query + part_query
        key_acc = key_acc + part_key
        value_acc = value_acc + part_value
        if offset + 1 < SPAN:
            key_cur, value_cur = passed_along((key_cur, value_cur), "cp", 1)
            key_acc, value_acc = shifted((key_acc, value_acc), "cp", 1)
    key_acc, value_acc = shifted((key_acc, value_acc), "cp", 1 - SPAN)
    key_sum, value_sum = lax.psum((key_acc, value_acc), "hd")
    grad_query_out = (
        (grad_query * scaling).astype(jnp.bfloat16).reshape(row_count, head_count * HDIM)
    )
    return (
        grad_query_out,
        (key_sum * scaling).astype(jnp.bfloat16),
        value_sum.astype(jnp.bfloat16),
    )


def solution(mesh):
    in_specs = (P("cp", "hd"), P("cp", None), P("cp", None), P("cp", "hd"), P("cp"))
    out_specs = (P("cp", "hd"), P("cp", None), P("cp", None))
    return jax.shard_map(body, mesh=mesh, in_specs=in_specs, out_specs=out_specs, check_vma=False)
```

profile of v0, /device:TPU:0, one launch (start us, length us, event | category | flops | bytes accessed | tf_op | source)
XLA Modules:
  0.0 189.4 jit_solution(17929398274000264187)
XLA Ops:
  7.2 2.5 %collective-permute-start = (bf16[512,128]{1,0:T(8,128)(2,1)}, bf16[512,128]{1,0:T(8,128)(2,1)S(1)}, u32[]{:S(2)}, u32[]{:S(2)}) collective-permute-start(bf16[512,128]{1,0:T(8,128)(2,1)} %param.6), channel_id=1, source_target_pairs={{0,2},{2,4},{4,6},{6,8},{8,10},{10,12},{12,14},{14,16},{16,18},{18... | collective-permute-start | bytes 393224 | tf_op jit(solution)/shard_map/ppermute | solution.py:18
  9.8 4.5 %collective-permute-start.7 = (bf16[512,128]{1,0:T(8,128)(2,1)}, bf16[512,128]{1,0:T(8,128)(2,1)S(1)}, u32[]{:S(2)}, u32[]{:S(2)}) collective-permute-start(bf16[512,128]{1,0:T(8,128)(2,1)} %param.7), channel_id=1, source_target_pairs={{0,2},{2,4},{4,6},{6,8},{8,10},{10,12},{12,14},{14,16},{16,18},{18... | collective-permute-start | bytes 393224 | tf_op jit(solution)/shard_map/ppermute | solution.py:18
  14.3 2.7 %compare_and_fusion.7 = (pred[512,512]{0,1:T(8,128)(4,1)S(1)}, pred[512,512]{0,1:T(8,128)(4,1)S(1)}, pred[512,512]{0,1:T(8,128)(4,1)S(1)}, pred[512,512]{0,1:T(8...) fusion(s32[512]{0:T(512)S(1)} %get-tuple-element.79, ...), kind=kLoop, calls=%fused_computation.162 | loop fusion | flops 6291456 | bytes 2115584 | tf_op jit(solution)/shard_map/and | solution.py:29
  17.1 0.6 fusion.40
  17.7 1.9 %collective-permute-start.1 = (bf16[512,128]{1,0:T(8,128)(2,1)S(1)}, bf16[512,128]{1,0:T(8,128)(2,1)S(1)}, u32[]{:S(2)}, u32[]{:S(2)}) collective-permute-start(bf16[512,128]{1,0:T(8,128)(2,1)S(1)} %collective-permute-done), channel_id=1, source_target_pairs={{0,2},{2,4},{4,6},{6,8},{8,10},{10,12},{12,14},{14,16},{16,18},{18... | collective-permute-start | bytes 393224 | tf_op jit(solution)/shard_map/ppermute | solution.py:18
  19.6 0.6 fusion.41
  20.2 3.6 %collective-permute-start.8 = (bf16[512,128]{1,0:T(8,128)(2,1)S(1)}, bf16[512,128]{1,0:T(8,128)(2,1)S(1)}, u32[]{:S(2)}, u32[]{:S(2)}) collective-permute-start(bf16[512,128]{1,0:T(8,128)(2,1)S(1)} %collective-permute-done.7), channel_id=1, source_target_pairs={{0,2},{2,4},{4,6},{6,8},{8,10},{10,12},{12,14},{14,16},{16,18},{18... | collective-permute-start | bytes 393224 | tf_op jit(solution)/shard_map/ppermute | solution.py:18
  23.7 1.9 %collective-permute-start.2 = (bf16[512,128]{1,0:T(8,128)(2,1)S(1)}, bf16[512,128]{1,0:T(8,128)(2,1)S(1)}, u32[]{:S(2)}, u32[]{:S(2)}) collective-permute-start(bf16[512,128]{1,0:T(8,128)(2,1)S(1)} %collective-permute-done.1), channel_id=1, source_target_pairs={{0,2},{2,4},{4,6},{6,8},{8,10},{10,12},{12,14},{14,16},{16,18},{18... | collective-permute-start | bytes 393224 | tf_op jit(solution)/shard_map/ppermute | solution.py:18
  25.7 0.6 fusion.42
  26.2 3.8 %collective-permute-start.9 = (bf16[512,128]{1,0:T(8,128)(2,1)S(1)}, bf16[512,128]{1,0:T(8,128)(2,1)S(1)}, u32[]{:S(2)}, u32[]{:S(2)}) collective-permute-start(bf16[512,128]{1,0:T(8,128)(2,1)S(1)} %collective-permute-done.8), channel_id=1, source_target_pairs={{0,2},{2,4},{4,6},{6,8},{8,10},{10,12},{12,14},{14,16},{16,18},{18... | collective-permute-start | bytes 393224 | tf_op jit(solution)/shard_map/ppermute | solution.py:18
  30.0 1.9 %collective-permute-start.3 = (bf16[512,128]{1,0:T(8,128)(2,1)S(1)}, bf16[512,128]{1,0:T(8,128)(2,1)S(1)}, u32[]{:S(2)}, u32[]{:S(2)}) collective-permute-start(bf16[512,128]{1,0:T(8,128)(2,1)S(1)} %collective-permute-done.2), channel_id=1, source_target_pairs={{0,2},{2,4},{4,6},{6,8},{8,10},{10,12},{12,14},{14,16},{16,18},{18... | collective-permute-start | bytes 393224 | tf_op jit(solution)/shard_map/ppermute | solution.py:18
  32.0 0.6 fusion.43
  32.5 4.4 %collective-permute-start.10 = (bf16[512,128]{1,0:T(8,128)(2,1)S(1)}, bf16[512,128]{1,0:T(8,128)(2,1)S(1)}, u32[]{:S(2)}, u32[]{:S(2)}) collective-permute-start(bf16[512,128]{1,0:T(8,128)(2,1)S(1)} %collective-permute-done.9), channel_id=1, source_target_pairs={{0,2},{2,4},{4,6},{6,8},{8,10},{10,12},{12,14},{14,16},{16,18},{18... | collective-permute-start | bytes 393224 | tf_op jit(solution)/shard_map/ppermute | solution.py:18
  36.9 1.9 %collective-permute-start.4 = (bf16[512,128]{1,0:T(8,128)(2,1)S(1)}, bf16[512,128]{1,0:T(8,128)(2,1)S(1)}, u32[]{:S(2)}, u32[]{:S(2)}) collective-permute-start(bf16[512,128]{1,0:T(8,128)(2,1)S(1)} %collective-permute-done.3), channel_id=1, source_target_pairs={{0,2},{2,4},{4,6},{6,8},{8,10},{10,12},{12,14},{14,16},{16,18},{18... | collective-permute-start | bytes 393224 | tf_op jit(solution)/shard_map/ppermute | solution.py:18
  38.9 0.6 fusion.44
  39.5 4.7 %collective-permute-start.11 = (bf16[512,128]{1,0:T(8,128)(2,1)S(1)}, bf16[512,128]{1,0:T(8,128)(2,1)S(1)}, u32[]{:S(2)}, u32[]{:S(2)}) collective-permute-start(bf16[512,128]{1,0:T(8,128)(2,1)S(1)} %collective-permute-done.10), channel_id=1, source_target_pairs={{0,2},{2,4},{4,6},{6,8},{8,10},{10,12},{12,14},{14,16},{16,18},{18... | collective-permute-start | bytes 393224 | tf_op jit(solution)/shard_map/ppermute | solution.py:18
  44.1 1.9 %collective-permute-start.5 = (bf16[512,128]{1,0:T(8,128)(2,1)S(1)}, bf16[512,128]{1,0:T(8,128)(2,1)S(1)}, u32[]{:S(2)}, u32[]{:S(2)}) collective-permute-start(bf16[512,128]{1,0:T(8,128)(2,1)S(1)} %collective-permute-done.4), channel_id=1, source_target_pairs={{0,2},{2,4},{4,6},{6,8},{8,10},{10,12},{12,14},{14,16},{16,18},{18... | collective-permute-start | bytes 393224 | tf_op jit(solution)/shard_map/ppermute | solution.py:18
  46.1 0.5 fusion.45
  46.6 4.7 %collective-permute-start.12 = (bf16[512,128]{1,0:T(8,128)(2,1)S(1)}, bf16[512,128]{1,0:T(8,128)(2,1)S(1)}, u32[]{:S(2)}, u32[]{:S(2)}) collective-permute-start(bf16[512,128]{1,0:T(8,128)(2,1)S(1)} %collective-permute-done.11), channel_id=1, source_target_pairs={{0,2},{2,4},{4,6},{6,8},{8,10},{10,12},{12,14},{14,16},{16,18},{18... | collective-permute-start | bytes 393224 | tf_op jit(solution)/shard_map/ppermute | solution.py:18
  51.3 1.9 %collective-permute-start.6 = (bf16[512,128]{1,0:T(8,128)(2,1)S(1)}, bf16[512,128]{1,0:T(8,128)(2,1)S(1)}, u32[]{:S(2)}, u32[]{:S(2)}) collective-permute-start(bf16[512,128]{1,0:T(8,128)(2,1)S(1)} %collective-permute-done.5), channel_id=1, source_target_pairs={{0,2},{2,4},{4,6},{6,8},{8,10},{10,12},{12,14},{14,16},{16,18},{18... | collective-permute-start | bytes 393224 | tf_op jit(solution)/shard_map/ppermute | solution.py:18
  53.2 0.6 fusion.46
  53.8 5.0 %collective-permute-start.13 = (bf16[512,128]{1,0:T(8,128)(2,1)S(1)}, bf16[512,128]{1,0:T(8,128)(2,1)S(1)}, u32[]{:S(2)}, u32[]{:S(2)}) collective-permute-start(bf16[512,128]{1,0:T(8,128)(2,1)S(1)} %collective-permute-done.12), channel_id=1, source_target_pairs={{0,2},{2,4},{4,6},{6,8},{8,10},{10,12},{12,14},{14,16},{16,18},{18... | collective-permute-start | bytes 393224 | tf_op jit(solution)/shard_map/ppermute | solution.py:18
  58.8 0.6 fusion.47
  59.4 0.9 fusion.21
  60.3 0.9 fusion.3
  61.3 0.9 fusion.6
  62.2 0.9 fusion.9
  63.1 2.1 %fusion.12 = (f32[2,512]{1,0:T(2,128)S(1)}, f32[2,512]{1,0:T(2,128)S(1)}, f32[512,512,2]{1,0,2:T(8,128)}) fusion(f32[512,512,2]{1,0,2:T(8,128)S(1)} %get-tuple-element.57, f32[2,512]{1,0:T(2,128)S(1)} %get-tuple-element.28, pred[512,512]{0,1:T(8,128)(4,1)S(1)} %get-tuple-element.42, bf16[512,128]{1,0:T(8,128)(2,1)S(1)} %collective-permute-done.9, ...), kind=kOutput, calls=%fused_computation.22 | convolution fusion | flops 137885696 | bytes 4861952 | tf_op jit(solution)/shard_map/thd,kd->htk/dot_general | solution.py:48
  65.3 2.1 %fusion.15 = (f32[2,512]{1,0:T(2,128)S(1)}, f32[2,512]{1,0:T(2,128)S(1)}, f32[512,512,2]{1,0,2:T(8,128)}) fusion(f32[512,512,2]{1,0,2:T(8,128)S(1)} %get-tuple-element.59, f32[2,512]{1,0:T(2,128)S(1)} %get-tuple-element.29, pred[512,512]{0,1:T(8,128)(4,1)S(1)} %get-tuple-element.41, bf16[512,128]{1,0:T(8,128)(2,1)S(1)} %collective-permute-done.8, ...), kind=kOutput, calls=%fused_computation.27 | convolution fusion | flops 137885696 | bytes 4861952 | tf_op jit(solution)/shard_map/thd,kd->htk/dot_general | solution.py:48
  67.4 2.2 %fusion.18 = (f32[2,512]{1,0:T(2,128)S(1)}, f32[2,512]{1,0:T(2,128)S(1)}, f32[512,512,2]{1,0,2:T(8,128)}) fusion(f32[512,512,2]{1,0,2:T(8,128)S(1)} %get-tuple-element.61, f32[2,512]{1,0:T(2,128)S(1)} %get-tuple-element.30, pred[512,512]{0,1:T(8,128)(4,1)S(1)} %get-tuple-element.47, bf16[512,128]{1,0:T(8,128)(2,1)S(1)} %collective-permute-done.7, ...), kind=kOutput, calls=%fused_computation.32 | convolution fusion | flops 137885696 | bytes 4861952 | tf_op jit(solution)/shard_map/thd,kd->htk/dot_general | solution.py:48
  69.6 2.1 %fusion = (f32[2,512]{1,0:T(2,128)S(1)}, f32[2,512]{1,0:T(2,128)S(1)}, f32[512,512,2]{1,0,2:T(8,128)}) fusion(f32[512,512,2]{1,0,2:T(8,128)S(1)} %get-tuple-element.49, f32[2,512]{1,0:T(2,128)S(1)} %get-tuple-element.24, pred[512,512]{0,1:T(8,128)(4,1)S(1)} %get-tuple-element.46, bf16[512,128]{1,0:T(8,128)(2,1)S(1)} %collective-permute-done.13, ...), kind=kOutput, calls=%fused_computation.2 | convolution fusion | flops 137885696 | bytes 4861952 | tf_op jit(solution)/shard_map/thd,kd->htk/dot_general | solution.py:48
  71.8 2.0 %fusion.5 = (bf16[2,512,512]{1,2,0:T(8,128)(2,1)S(1)}, bf16[2,512,512]{1,2,0:T(8,128)(2,1)S(1)}, bf16[2,512,512]{1,2,0:T(8,128)(2,1)S(1)}) fusion(f32[512,512,2]{1,0,2:T(8,128)S(1)} %get-tuple-element.65, f32[512,512,2]{1,0,2:T(8,128)S(1)} %get-tuple-element.51, f32[2,512]{1,0:T(2,128)S(1)} %add_divide_fusion, f32[2,512]{1,0:T(2,128)S(1)} %get-tuple-element.22, ...), kind=kLoop, calls=%fused_computation.9 | loop fusion | flops 9437184 | bytes 16523264 | tf_op jit(solution)/shard_map/convert_element_type | solution.py:80
  74.2 1.1 convolution_bitcast_fusion.15
  75.4 1.2 convolution_bitcast_fusion.7
  76.6 5.5 %fusion.2 = (bf16[2,512,512]{1,2,0:T(8,128)(2,1)S(1)}, bf16[2,512,512]{1,2,0:T(8,128)(2,1)S(1)}, bf16[2,512,512]{1,2,0:T(8,128)(2,1)S(1)}, bf16[2,512,512]{1,2,0:T(8,128)(2,1)S(1)}, bf16[2,512,512]{1,2,0:T(8,128)(2,1)S(1)}) fusion(f32[512,512,2]{1,0,2:T(8,128)} %get-tuple-element.64, f32[512,512,2]{1,0,2:T(8,128)S(1)} %get-tuple-element.49, ...), kind=kLoop, calls=%fused_computation.4 | loop fusion | flops 15728640 | bytes 27533312 | tf_op jit(solution)/shard_map/convert_element_type | solution.py:80
  84.8 2.8 %collective-permute-start.22 = (f32[512,128]{1,0:T(8,128)S(1)}, f32[512,128]{1,0:T(8,128)S(1)}, u32[]{:S(2)}, u32[]{:S(2)}) collective-permute-start(f32[512,128]{1,0:T(8,128)S(1)} %copy-done.27), channel_id=1, source_target_pairs={{0,2},{2,4},{4,6},{6,8},{8,10},{10,12},{12,14},{14,16},{16,18},{18... | collective-permute-start | bytes 786440 | tf_op jit(solution)/shard_map/ppermute | solution.py:23
  90.1 1.4 fusion.66
  91.6 1.7 collective-permute-done.22
  93.3 0.6 fusion.67
  94.0 0.7 collective-permute-start.23
  95.3 4.8 %collective-permute-done.15 = f32[512,128]{1,0:T(8,128)S(1)} collective-permute-done((f32[512,128]{1,0:T(8,128)S(1)}, f32[512,128]{1,0:T(8,128)S(1)}, u32[]{:S(2)}, u32[]{:S(2)}) %collective-permute-start.15) | collective-permute-done | bytes 262176 | tf_op jit(solution)/shard_map/ppermute | solution.py:23
  100.2 2.7 %collective-permute-done.23 = f32[512,128]{1,0:T(8,128)S(1)} collective-permute-done((f32[512,128]{1,0:T(8,128)S(1)}, f32[512,128]{1,0:T(8,128)S(1)}, u32[]{:S(2)}, u32[]{:S(2)}) %collective-permute-start.23) | collective-permute-done | bytes 262176 | tf_op jit(solution)/shard_map/ppermute | solution.py:23
  103.0 0.5 convolution_bitcast_fusion.4
  103.6 5.1 %collective-permute-done.16 = f32[512,128]{1,0:T(8,128)S(1)} collective-permute-done((f32[512,128]{1,0:T(8,128)S(1)}, f32[512,128]{1,0:T(8,128)S(1)}, u32[]{:S(2)}, u32[]{:S(2)}) %collective-permute-start.16) | collective-permute-done | bytes 262176 | tf_op jit(solution)/shard_map/ppermute | solution.py:23
  108.8 2.7 %collective-permute-done.24 = f32[512,128]{1,0:T(8,128)S(1)} collective-permute-done((f32[512,128]{1,0:T(8,128)S(1)}, f32[512,128]{1,0:T(8,128)S(1)}, u32[]{:S(2)}, u32[]{:S(2)}) %collective-permute-start.24) | collective-permute-done | bytes 262176 | tf_op jit(solution)/shard_map/ppermute | solution.py:23
  111.6 0.5 convolution_bitcast_fusion.3
  112.1 5.1 %collective-permute-done.17 = f32[512,128]{1,0:T(8,128)S(1)} collective-permute-done((f32[512,128]{1,0:T(8,128)S(1)}, f32[512,128]{1,0:T(8,128)S(1)}, u32[]{:S(2)}, u32[]{:S(2)}) %collective-permute-start.17) | collective-permute-done | bytes 262176 | tf_op jit(solution)/shard_map/ppermute | solution.py:23
  117.4 2.7 %collective-permute-done.25 = f32[512,128]{1,0:T(8,128)S(1)} collective-permute-done((f32[512,128]{1,0:T(8,128)S(1)}, f32[512,128]{1,0:T(8,128)S(1)}, u32[]{:S(2)}, u32[]{:S(2)}) %collective-permute-start.25) | collective-permute-done | bytes 262176 | tf_op jit(solution)/shard_map/ppermute | solution.py:23
  120.2 0.5 convolution_bitcast_fusion.2
  120.7 5.1 %collective-permute-done.18 = f32[512,128]{1,0:T(8,128)S(1)} collective-permute-done((f32[512,128]{1,0:T(8,128)S(1)}, f32[512,128]{1,0:T(8,128)S(1)}, u32[]{:S(2)}, u32[]{:S(2)}) %collective-permute-start.18) | collective-permute-done | bytes 262176 | tf_op jit(solution)/shard_map/ppermute | solution.py:23
  125.9 2.7 %collective-permute-done.26 = f32[512,128]{1,0:T(8,128)S(1)} collective-permute-done((f32[512,128]{1,0:T(8,128)S(1)}, f32[512,128]{1,0:T(8,128)S(1)}, u32[]{:S(2)}, u32[]{:S(2)}) %collective-permute-start.26) | collective-permute-done | bytes 262176 | tf_op jit(solution)/shard_map/ppermute | solution.py:23
  128.8 0.5 convolution_bitcast_fusion.1
  129.3 5.1 %collective-permute-done.19 = f32[512,128]{1,0:T(8,128)S(1)} collective-permute-done((f32[512,128]{1,0:T(8,128)S(1)}, f32[512,128]{1,0:T(8,128)S(1)}, u32[]{:S(2)}, u32[]{:S(2)}) %collective-permute-start.19) | collective-permute-done | bytes 262176 | tf_op jit(solution)/shard_map/ppermute | solution.py:23
  134.5 2.8 %collective-permute-done.27 = f32[512,128]{1,0:T(8,128)S(1)} collective-permute-done((f32[512,128]{1,0:T(8,128)S(1)}, f32[512,128]{1,0:T(8,128)S(1)}, u32[]{:S(2)}, u32[]{:S(2)}) %collective-permute-start.27) | collective-permute-done | bytes 262176 | tf_op jit(solution)/shard_map/ppermute | solution.py:23
  137.5 0.5 convolution_bitcast_fusion
  138.0 6.5 %collective-permute-done.20 = f32[512,128]{1,0:T(8,128)S(1)} collective-permute-done((f32[512,128]{1,0:T(8,128)S(1)}, f32[512,128]{1,0:T(8,128)S(1)}, u32[]{:S(2)}, u32[]{:S(2)}) %collective-permute-start.20) | collective-permute-done | bytes 262176 | tf_op jit(solution)/shard_map/ppermute | solution.py:23
  144.6 4.2 %collective-permute-done.28 = f32[512,128]{1,0:T(8,128)S(1)} collective-permute-done((f32[512,128]{1,0:T(8,128)S(1)}, f32[512,128]{1,0:T(8,128)S(1)}, u32[]{:S(2)}, u32[]{:S(2)}) %collective-permute-start.28) | collective-permute-done | bytes 262176 | tf_op jit(solution)/shard_map/ppermute | solution.py:23
  149.2 0.8 copy.56
  150.1 3.3 %collective-permute-done.21 = f32[512,128]{1,0:T(8,128)S(1)} collective-permute-done((f32[512,128]{1,0:T(8,128)S(1)}, f32[512,128]{1,0:T(8,128)S(1)}, u32[]{:S(2)}, u32[]{:S(2)}) %collective-permute-start.21) | collective-permute-done | bytes 262176 | tf_op jit(solution)/shard_map/ppermute | solution.py:23
  153.3 0.7 copy-done.14
  154.0 3.1 %collective-permute-done.29 = f32[512,128]{1,0:T(8,128)S(1)} collective-permute-done((f32[512,128]{1,0:T(8,128)S(1)}, f32[512,128]{1,0:T(8,128)S(1)}, u32[]{:S(2)}, u32[]{:S(2)}) %collective-permute-start.29) | collective-permute-done | bytes 262176 | tf_op jit(solution)/shard_map/ppermute | solution.py:23
  157.1 16.3 %all-reduce.4 = bf16[512,128]{1,0:T(8,128)(2,1)} all-reduce(f32[512,128]{1,0:T(8,128)S(1)} %collective-permute-done.29), channel_id=1, replica_groups=mesh['cp'=16,'hd'=2] {'hd'}, use_global_device_ids=true, to_apply=%region_25.26 | all-reduce | flops 65536 | bytes 393216 | tf_op jit(solution)/shard_map/psum | solution.py:150
  173.4 7.6 %all-reduce.3.cloned.1.call-done = f32[512,128]{1,0:T(8,128)} async-done(((f32[512,128]{1,0:T(8,128)}), f32[512,128]{1,0:T(8,128)}) %all-reduce.3.cloned.1.call-update) | async-done | bytes 262160 | tf_op jit(solution)/shard_map/psum | solution.py:150
  181.0 1.6 multiply_convert_fusion
  (122 shorter events, 7.8 us)
Async XLA Ops:
  7.2 52.2 %copy-start = (bf16[512,256]{1,0:T(8,128)(2,1)S(1)}, bf16[512,256]{1,0:T(8,128)(2,1)}, u32[]{:S(2)}) copy-start(bf16[512,256]{1,0:T(8,128)(2,1)} %param.8) | copy-start | bytes 786436
  7.2 9.9 %copy-start.23 = (bf16[512,128]{1,0:T(8,128)(2,1)S(1)}, bf16[512,128]{1,0:T(8,128)(2,1)}, u32[]{:S(2)}) copy-start(bf16[512,128]{1,0:T(8,128)(2,1)} %param.6) | copy-start | bytes 393220
  7.2 9.9 %copy-start.1 = (bf16[512,256]{1,0:T(8,128)(2,1)S(1)}, bf16[512,256]{1,0:T(8,128)(2,1)}, u32[]{:S(2)}) copy-start(bf16[512,256]{1,0:T(8,128)(2,1)} %param.5) | copy-start | bytes 786436
  7.2 173.8 %all-reduce.3.cloned.1.call-start = ((), (), s32[]{:S(2)}) async-start(), calls=%async_computation | async-start | bytes 524288 | tf_op jit(solution)/shard_map/psum | solution.py:150
  7.2 10.4 %collective-permute-start = (bf16[512,128]{1,0:T(8,128)(2,1)}, bf16[512,128]{1,0:T(8,128)(2,1)S(1)}, u32[]{:S(2)}, u32[]{:S(2)}) collective-permute-start(bf16[512,128]{1,0:T(8,128)(2,1)} %param.6), channel_id=1, source_target_pairs={{0,2},{2,4},{4,6},{6,8},{8,10},{10,12},{12,14},{14,16},{16,18},{18... | collective-permute-start | bytes 393224 | tf_op jit(solution)/shard_map/ppermute | solution.py:18
  9.8 10.4 %collective-permute-start.7 = (bf16[512,128]{1,0:T(8,128)(2,1)}, bf16[512,128]{1,0:T(8,128)(2,1)S(1)}, u32[]{:S(2)}, u32[]{:S(2)}) collective-permute-start(bf16[512,128]{1,0:T(8,128)(2,1)} %param.7), channel_id=1, source_target_pairs={{0,2},{2,4},{4,6},{6,8},{8,10},{10,12},{12,14},{14,16},{16,18},{18... | collective-permute-start | bytes 393224 | tf_op jit(solution)/shard_map/ppermute | solution.py:18
  17.0 45.2 %copy-start.6 = (pred[512,512]{0,1:T(8,128)(4,1)}, pred[512,512]{0,1:T(8,128)(4,1)S(1)}, u32[]{:S(2)}) copy-start(pred[512,512]{0,1:T(8,128)(4,1)S(1)} %get-tuple-element.43) | copy-start | bytes 786436
  17.0 46.1 %copy-start.8 = (pred[512,512]{0,1:T(8,128)(4,1)}, pred[512,512]{0,1:T(8,128)(4,1)S(1)}, u32[]{:S(2)}) copy-start(pred[512,512]{0,1:T(8,128)(4,1)S(1)} %get-tuple-element.42) | copy-start | bytes 786436
  17.0 48.2 %copy-start.10 = (pred[512,512]{0,1:T(8,128)(4,1)}, pred[512,512]{0,1:T(8,128)(4,1)S(1)}, u32[]{:S(2)}) copy-start(pred[512,512]{0,1:T(8,128)(4,1)S(1)} %get-tuple-element.41) | copy-start | bytes 786436
  17.0 50.4 %copy-start.12 = (pred[512,512]{0,1:T(8,128)(4,1)}, pred[512,512]{0,1:T(8,128)(4,1)S(1)}, u32[]{:S(2)}) copy-start(pred[512,512]{0,1:T(8,128)(4,1)S(1)} %get-tuple-element.47) | copy-start | bytes 786436
  17.1 54.7 %copy-start.2 = (pred[512,512]{0,1:T(8,128)(4,1)}, pred[512,512]{0,1:T(8,128)(4,1)S(1)}, u32[]{:S(2)}) copy-start(pred[512,512]{0,1:T(8,128)(4,1)S(1)} %get-tuple-element.45) | copy-start | bytes 786436
  17.1 54.7 %copy-start.4 = (pred[512,512]{0,1:T(8,128)(4,1)}, pred[512,512]{0,1:T(8,128)(4,1)S(1)}, u32[]{:S(2)}) copy-start(pred[512,512]{0,1:T(8,128)(4,1)S(1)} %get-tuple-element.44) | copy-start | bytes 786436
  17.7 6.1 %collective-permute-start.1 = (bf16[512,128]{1,0:T(8,128)(2,1)S(1)}, bf16[512,128]{1,0:T(8,128)(2,1)S(1)}, u32[]{:S(2)}, u32[]{:S(2)}) collective-permute-start(bf16[512,128]{1,0:T(8,128)(2,1)S(1)} %collective-permute-done), channel_id=1, source_target_pairs={{0,2},{2,4},{4,6},{6,8},{8,10},{10,12},{12,14},{14,16},{16,18},{18... | collective-permute-start | bytes 393224 | tf_op jit(solution)/shard_map/ppermute | solution.py:18
  20.2 6.1 %collective-permute-start.8 = (bf16[512,128]{1,0:T(8,128)(2,1)S(1)}, bf16[512,128]{1,0:T(8,128)(2,1)S(1)}, u32[]{:S(2)}, u32[]{:S(2)}) collective-permute-start(bf16[512,128]{1,0:T(8,128)(2,1)S(1)} %collective-permute-done.7), channel_id=1, source_target_pairs={{0,2},{2,4},{4,6},{6,8},{8,10},{10,12},{12,14},{14,16},{16,18},{18... | collective-permute-start | bytes 393224 | tf_op jit(solution)/shard_map/ppermute | solution.py:18
  23.7 6.3 %collective-permute-start.2 = (bf16[512,128]{1,0:T(8,128)(2,1)S(1)}, bf16[512,128]{1,0:T(8,128)(2,1)S(1)}, u32[]{:S(2)}, u32[]{:S(2)}) collective-permute-start(bf16[512,128]{1,0:T(8,128)(2,1)S(1)} %collective-permute-done.1), channel_id=1, source_target_pairs={{0,2},{2,4},{4,6},{6,8},{8,10},{10,12},{12,14},{14,16},{16,18},{18... | collective-permute-start | bytes 393224 | tf_op jit(solution)/shard_map/ppermute | solution.py:18
  26.2 6.3 %collective-permute-start.9 = (bf16[512,128]{1,0:T(8,128)(2,1)S(1)}, bf16[512,128]{1,0:T(8,128)(2,1)S(1)}, u32[]{:S(2)}, u32[]{:S(2)}) collective-permute-start(bf16[512,128]{1,0:T(8,128)(2,1)S(1)} %collective-permute-done.8), channel_id=1, source_target_pairs={{0,2},{2,4},{4,6},{6,8},{8,10},{10,12},{12,14},{14,16},{16,18},{18... | collective-permute-start | bytes 393224 | tf_op jit(solution)/shard_map/ppermute | solution.py:18
  30.0 9.4 %copy-start.15 = (bf16[512,128]{1,0:T(8,128)(2,1)}, bf16[512,128]{1,0:T(8,128)(2,1)S(1)}, u32[]{:S(2)}) copy-start(bf16[512,128]{1,0:T(8,128)(2,1)S(1)} %collective-permute-done.2) | copy-start | bytes 393220
  30.0 6.9 %collective-permute-start.3 = (bf16[512,128]{1,0:T(8,128)(2,1)S(1)}, bf16[512,128]{1,0:T(8,128)(2,1)S(1)}, u32[]{:S(2)}, u32[]{:S(2)}) collective-permute-start(bf16[512,128]{1,0:T(8,128)(2,1)S(1)} %collective-permute-done.2), channel_id=1, source_target_pairs={{0,2},{2,4},{4,6},{6,8},{8,10},{10,12},{12,14},{14,16},{16,18},{18... | collective-permute-start | bytes 393224 | tf_op jit(solution)/shard_map/ppermute | solution.py:18
  32.5 6.9 %collective-permute-start.10 = (bf16[512,128]{1,0:T(8,128)(2,1)S(1)}, bf16[512,128]{1,0:T(8,128)(2,1)S(1)}, u32[]{:S(2)}, u32[]{:S(2)}) collective-permute-start(bf16[512,128]{1,0:T(8,128)(2,1)S(1)} %collective-permute-done.9), channel_id=1, source_target_pairs={{0,2},{2,4},{4,6},{6,8},{8,10},{10,12},{12,14},{14,16},{16,18},{18... | collective-permute-start | bytes 393224 | tf_op jit(solution)/shard_map/ppermute | solution.py:18
  36.9 9.7 %copy-start.17 = (bf16[512,128]{1,0:T(8,128)(2,1)}, bf16[512,128]{1,0:T(8,128)(2,1)S(1)}, u32[]{:S(2)}) copy-start(bf16[512,128]{1,0:T(8,128)(2,1)S(1)} %collective-permute-done.3) | copy-start | bytes 393220
  36.9 7.2 %collective-permute-start.4 = (bf16[512,128]{1,0:T(8,128)(2,1)S(1)}, bf16[512,128]{1,0:T(8,128)(2,1)S(1)}, u32[]{:S(2)}, u32[]{:S(2)}) collective-permute-start(bf16[512,128]{1,0:T(8,128)(2,1)S(1)} %collective-permute-done.3), channel_id=1, source_target_pairs={{0,2},{2,4},{4,6},{6,8},{8,10},{10,12},{12,14},{14,16},{16,18},{18... | collective-permute-start | bytes 393224 | tf_op jit(solution)/shard_map/ppermute | solution.py:18
  39.5 7.2 %collective-permute-start.11 = (bf16[512,128]{1,0:T(8,128)(2,1)S(1)}, bf16[512,128]{1,0:T(8,128)(2,1)S(1)}, u32[]{:S(2)}, u32[]{:S(2)}) collective-permute-start(bf16[512,128]{1,0:T(8,128)(2,1)S(1)} %collective-permute-done.10), channel_id=1, source_target_pairs={{0,2},{2,4},{4,6},{6,8},{8,10},{10,12},{12,14},{14,16},{16,18},{18... | collective-permute-start | bytes 393224 | tf_op jit(solution)/shard_map/ppermute | solution.py:18
  44.1 9.7 %copy-start.19 = (bf16[512,128]{1,0:T(8,128)(2,1)}, bf16[512,128]{1,0:T(8,128)(2,1)S(1)}, u32[]{:S(2)}) copy-start(bf16[512,128]{1,0:T(8,128)(2,1)S(1)} %collective-permute-done.4) | copy-start | bytes 393220
  44.1 7.2 %collective-permute-start.5 = (bf16[512,128]{1,0:T(8,128)(2,1)S(1)}, bf16[512,128]{1,0:T(8,128)(2,1)S(1)}, u32[]{:S(2)}, u32[]{:S(2)}) collective-permute-start(bf16[512,128]{1,0:T(8,128)(2,1)S(1)} %collective-permute-done.4), channel_id=1, source_target_pairs={{0,2},{2,4},{4,6},{6,8},{8,10},{10,12},{12,14},{14,16},{16,18},{18... | collective-permute-start | bytes 393224 | tf_op jit(solution)/shard_map/ppermute | solution.py:18
  46.6 7.2 %collective-permute-start.12 = (bf16[512,128]{1,0:T(8,128)(2,1)S(1)}, bf16[512,128]{1,0:T(8,128)(2,1)S(1)}, u32[]{:S(2)}, u32[]{:S(2)}) collective-permute-start(bf16[512,128]{1,0:T(8,128)(2,1)S(1)} %collective-permute-done.11), channel_id=1, source_target_pairs={{0,2},{2,4},{4,6},{6,8},{8,10},{10,12},{12,14},{14,16},{16,18},{18... | collective-permute-start | bytes 393224 | tf_op jit(solution)/shard_map/ppermute | solution.py:18
  51.3 8.1 %copy-start.21 = (bf16[512,128]{1,0:T(8,128)(2,1)}, bf16[512,128]{1,0:T(8,128)(2,1)S(1)}, u32[]{:S(2)}) copy-start(bf16[512,128]{1,0:T(8,128)(2,1)S(1)} %collective-permute-done.5) | copy-start | bytes 393220
  51.3 7.5 %collective-permute-start.6 = (bf16[512,128]{1,0:T(8,128)(2,1)S(1)}, bf16[512,128]{1,0:T(8,128)(2,1)S(1)}, u32[]{:S(2)}, u32[]{:S(2)}) collective-permute-start(bf16[512,128]{1,0:T(8,128)(2,1)S(1)} %collective-permute-done.5), channel_id=1, source_target_pairs={{0,2},{2,4},{4,6},{6,8},{8,10},{10,12},{12,14},{14,16},{16,18},{18... | collective-permute-start | bytes 393224 | tf_op jit(solution)/shard_map/ppermute | solution.py:18
  53.8 5.6 %copy-start.28 = (bf16[512,128]{1,0:T(8,128)(2,1)S(1)}, bf16[512,128]{1,0:T(8,128)(2,1)}, u32[]{:S(2)}) copy-start(bf16[512,128]{1,0:T(8,128)(2,1)} %param.7) | copy-start | bytes 393220
  53.8 15.7 %collective-permute-start.13 = (bf16[512,128]{1,0:T(8,128)(2,1)S(1)}, bf16[512,128]{1,0:T(8,128)(2,1)S(1)}, u32[]{:S(2)}, u32[]{:S(2)}) collective-permute-start(bf16[512,128]{1,0:T(8,128)(2,1)S(1)} %collective-permute-done.12), channel_id=1, source_target_pairs={{0,2},{2,4},{4,6},{6,8},{8,10},{10,12},{12,14},{14,16},{16,18},{18... | collective-permute-start | bytes 393224 | tf_op jit(solution)/shard_map/ppermute | solution.py:18
  58.8 1.5 copy-start.25
  71.8 2.0 %copy-start.24 = (bf16[512,128]{1,0:T(8,128)(2,1)S(1)}, bf16[512,128]{1,0:T(8,128)(2,1)}, u32[]{:S(2)}) copy-start(bf16[512,128]{1,0:T(8,128)(2,1)} %param.6) | copy-start | bytes 393220
  76.6 13.5 %collective-permute-start.14 = (f32[512,128]{1,0:T(8,128)}, f32[512,128]{1,0:T(8,128)}, u32[]{:S(2)}, u32[]{:S(2)}) collective-permute-start(f32[512,128]{1,0:T(8,128)} %convolution_bitcast_fusion.15), channel_id=1, source_target_pairs={{0,2},{2,4},{4,6},{6,8},{8,10},{10,12},{12,14},{14,16},{16,18},{18... | collective-permute-start | bytes 786440 | tf_op jit(solution)/shard_map/ppermute | solution.py:23
  83.5 1.3 copy-start.27
  84.8 8.5 %collective-permute-start.22 = (f32[512,128]{1,0:T(8,128)S(1)}, f32[512,128]{1,0:T(8,128)S(1)}, u32[]{:S(2)}, u32[]{:S(2)}) collective-permute-start(f32[512,128]{1,0:T(8,128)S(1)} %copy-done.27), channel_id=1, source_target_pairs={{0,2},{2,4},{4,6},{6,8},{8,10},{10,12},{12,14},{14,16},{16,18},{18... | collective-permute-start | bytes 786440 | tf_op jit(solution)/shard_map/ppermute | solution.py:23
  87.6 0.9 copy-start.16
  87.9 0.9 copy-start.18
  88.5 0.9 copy-start.20
  88.9 0.9 copy-start.22
  89.8 3.6 %copy-start.13 = (pred[512,512]{0,1:T(8,128)(4,1)S(1)}, pred[512,512]{0,1:T(8,128)(4,1)}, u32[]{:S(2)}) copy-start(pred[512,512]{0,1:T(8,128)(4,1)} %copy-done.12) | copy-start | bytes 786436
  91.5 3.2 %copy-start.11 = (pred[512,512]{0,1:T(8,128)(4,1)S(1)}, pred[512,512]{0,1:T(8,128)(4,1)}, u32[]{:S(2)}) copy-start(pred[512,512]{0,1:T(8,128)(4,1)} %copy-done.10) | copy-start | bytes 786436
  91.6 8.5 %collective-permute-start.15 = (f32[512,128]{1,0:T(8,128)S(1)}, f32[512,128]{1,0:T(8,128)S(1)}, u32[]{:S(2)}, u32[]{:S(2)}) collective-permute-start(f32[512,128]{1,0:T(8,128)S(1)} %fusion.66), channel_id=1, source_target_pairs={{0,2},{2,4},{4,6},{6,8},{8,10},{10,12},{12,14},{14,16},{16,18},{18... | collective-permute-start | bytes 786440 | tf_op jit(solution)/shard_map/ppermute | solution.py:23
  94.0 9.0 %copy-start.9 = (pred[512,512]{0,1:T(8,128)(4,1)S(1)}, pred[512,512]{0,1:T(8,128)(4,1)}, u32[]{:S(2)}) copy-start(pred[512,512]{0,1:T(8,128)(4,1)} %copy-done.8) | copy-start | bytes 786436
  94.0 8.9 %collective-permute-start.23 = (f32[512,128]{1,0:T(8,128)S(1)}, f32[512,128]{1,0:T(8,128)S(1)}, u32[]{:S(2)}, u32[]{:S(2)}) collective-permute-start(f32[512,128]{1,0:T(8,128)S(1)} %fusion.67), channel_id=1, source_target_pairs={{0,2},{2,4},{4,6},{6,8},{8,10},{10,12},{12,14},{14,16},{16,18},{18... | collective-permute-start | bytes 786440 | tf_op jit(solution)/shard_map/ppermute | solution.py:23
  100.1 8.5 %collective-permute-start.16 = (f32[512,128]{1,0:T(8,128)S(1)}, f32[512,128]{1,0:T(8,128)S(1)}, u32[]{:S(2)}, u32[]{:S(2)}) collective-permute-start(f32[512,128]{1,0:T(8,128)S(1)} %add.397), channel_id=1, source_target_pairs={{0,2},{2,4},{4,6},{6,8},{8,10},{10,12},{12,14},{14,16},{16,18},{18... | collective-permute-start | bytes 786440 | tf_op jit(solution)/shard_map/ppermute | solution.py:23
  102.9 8.7 %copy-start.7 = (pred[512,512]{0,1:T(8,128)(4,1)S(1)}, pred[512,512]{0,1:T(8,128)(4,1)}, u32[]{:S(2)}) copy-start(pred[512,512]{0,1:T(8,128)(4,1)} %copy-done.6) | copy-start | bytes 786436
  102.9 8.5 %collective-permute-start.24 = (f32[512,128]{1,0:T(8,128)S(1)}, f32[512,128]{1,0:T(8,128)S(1)}, u32[]{:S(2)}, u32[]{:S(2)}) collective-permute-start(f32[512,128]{1,0:T(8,128)S(1)} %add.404), channel_id=1, source_target_pairs={{0,2},{2,4},{4,6},{6,8},{8,10},{10,12},{12,14},{14,16},{16,18},{18... | collective-permute-start | bytes 786440 | tf_op jit(solution)/shard_map/ppermute | solution.py:23
  108.7 8.5 %collective-permute-start.17 = (f32[512,128]{1,0:T(8,128)S(1)}, f32[512,128]{1,0:T(8,128)S(1)}, u32[]{:S(2)}, u32[]{:S(2)}) collective-permute-start(f32[512,128]{1,0:T(8,128)S(1)} %add.398), channel_id=1, source_target_pairs={{0,2},{2,4},{4,6},{6,8},{8,10},{10,12},{12,14},{14,16},{16,18},{18... | collective-permute-start | bytes 786440 | tf_op jit(solution)/shard_map/ppermute | solution.py:23
  111.5 8.7 %copy-start.5 = (pred[512,512]{0,1:T(8,128)(4,1)S(1)}, pred[512,512]{0,1:T(8,128)(4,1)}, u32[]{:S(2)}) copy-start(pred[512,512]{0,1:T(8,128)(4,1)} %copy-done.4) | copy-start | bytes 786436
  111.5 8.5 %collective-permute-start.25 = (f32[512,128]{1,0:T(8,128)S(1)}, f32[512,128]{1,0:T(8,128)S(1)}, u32[]{:S(2)}, u32[]{:S(2)}) collective-permute-start(f32[512,128]{1,0:T(8,128)S(1)} %add.405), channel_id=1, source_target_pairs={{0,2},{2,4},{4,6},{6,8},{8,10},{10,12},{12,14},{14,16},{16,18},{18... | collective-permute-start | bytes 786440 | tf_op jit(solution)/shard_map/ppermute | solution.py:23
  117.3 8.5 %collective-permute-start.18 = (f32[512,128]{1,0:T(8,128)S(1)}, f32[512,128]{1,0:T(8,128)S(1)}, u32[]{:S(2)}, u32[]{:S(2)}) collective-permute-start(f32[512,128]{1,0:T(8,128)S(1)} %add.399), channel_id=1, source_target_pairs={{0,2},{2,4},{4,6},{6,8},{8,10},{10,12},{12,14},{14,16},{16,18},{18... | collective-permute-start | bytes 786440 | tf_op jit(solution)/shard_map/ppermute | solution.py:23
  120.1 8.7 %copy-start.3 = (pred[512,512]{0,1:T(8,128)(4,1)S(1)}, pred[512,512]{0,1:T(8,128)(4,1)}, u32[]{:S(2)}) copy-start(pred[512,512]{0,1:T(8,128)(4,1)} %copy-done.2) | copy-start | bytes 786436
  120.1 8.5 %collective-permute-start.26 = (f32[512,128]{1,0:T(8,128)S(1)}, f32[512,128]{1,0:T(8,128)S(1)}, u32[]{:S(2)}, u32[]{:S(2)}) collective-permute-start(f32[512,128]{1,0:T(8,128)S(1)} %add.406), channel_id=1, source_target_pairs={{0,2},{2,4},{4,6},{6,8},{8,10},{10,12},{12,14},{14,16},{16,18},{18... | collective-permute-start | bytes 786440 | tf_op jit(solution)/shard_map/ppermute | solution.py:23
  125.9 8.5 %collective-permute-start.19 = (f32[512,128]{1,0:T(8,128)S(1)}, f32[512,128]{1,0:T(8,128)S(1)}, u32[]{:S(2)}, u32[]{:S(2)}) collective-permute-start(f32[512,128]{1,0:T(8,128)S(1)} %add.400), channel_id=1, source_target_pairs={{0,2},{2,4},{4,6},{6,8},{8,10},{10,12},{12,14},{14,16},{16,18},{18... | collective-permute-start | bytes 786440 | tf_op jit(solution)/shard_map/ppermute | solution.py:23
  128.7 8.6 %collective-permute-start.27 = (f32[512,128]{1,0:T(8,128)S(1)}, f32[512,128]{1,0:T(8,128)S(1)}, u32[]{:S(2)}, u32[]{:S(2)}) collective-permute-start(f32[512,128]{1,0:T(8,128)S(1)} %add.407), channel_id=1, source_target_pairs={{0,2},{2,4},{4,6},{6,8},{8,10},{10,12},{12,14},{14,16},{16,18},{18... | collective-permute-start | bytes 786440 | tf_op jit(solution)/shard_map/ppermute | solution.py:23
  134.4 10.0 %collective-permute-start.20 = (f32[512,128]{1,0:T(8,128)S(1)}, f32[512,128]{1,0:T(8,128)S(1)}, u32[]{:S(2)}, u32[]{:S(2)}) collective-permute-start(f32[512,128]{1,0:T(8,128)S(1)} %add.401), channel_id=1, source_target_pairs={{0,2},{2,4},{4,6},{6,8},{8,10},{10,12},{12,14},{14,16},{16,18},{18... | collective-permute-start | bytes 786440 | tf_op jit(solution)/shard_map/ppermute | solution.py:23
  137.4 11.5 %copy-start.26 = (bf16[512,128]{1,0:T(8,128)(2,1)S(1)}, bf16[512,128]{1,0:T(8,128)(2,1)}, u32[]{:S(2)}) copy-start(bf16[512,128]{1,0:T(8,128)(2,1)} %copy-done.25) | copy-start | bytes 393220
  137.4 11.3 %collective-permute-start.28 = (f32[512,128]{1,0:T(8,128)S(1)}, f32[512,128]{1,0:T(8,128)S(1)}, u32[]{:S(2)}, u32[]{:S(2)}) collective-permute-start(f32[512,128]{1,0:T(8,128)S(1)} %add.408), channel_id=1, source_target_pairs={{0,2},{2,4},{4,6},{6,8},{8,10},{10,12},{12,14},{14,16},{16,18},{18... | collective-permute-start | bytes 786440 | tf_op jit(solution)/shard_map/ppermute | solution.py:23
  144.5 8.8 %collective-permute-start.21 = (f32[512,128]{1,0:T(8,128)S(1)}, f32[512,128]{1,0:T(8,128)S(1)}, u32[]{:S(2)}, u32[]{:S(2)}) collective-permute-start(f32[512,128]{1,0:T(8,128)S(1)} %add.402), channel_id=1, source_target_pairs={{0,18},{2,20},{4,22},{6,24},{8,26},{10,28},{12,30},{14,0},{16,2},{... | collective-permute-start | bytes 786440 | tf_op jit(solution)/shard_map/ppermute | solution.py:23
  148.8 8.4 %collective-permute-start.29 = (f32[512,128]{1,0:T(8,128)S(1)}, f32[512,128]{1,0:T(8,128)S(1)}, u32[]{:S(2)}, u32[]{:S(2)}) collective-permute-start(f32[512,128]{1,0:T(8,128)S(1)} %add.409), channel_id=1, source_target_pairs={{0,18},{2,20},{4,22},{6,24},{8,26},{10,28},{12,30},{14,0},{16,2},{... | collective-permute-start | bytes 786440 | tf_op jit(solution)/shard_map/ppermute | solution.py:23
  153.3 0.7 copy-start.14
Sparse Core Ops, SparseCore 0:
  154.2 26.7 all-reduce.2
where the time goes:
time: 190 us; the launch traced here: 189 us
  waiting for transfers between devices  65.4 us (34%)
  starting transfers between devices  48.9 us (26%)
  matrix products  29.5 us (16%)
  blocking collectives  16.3 us (9%)
  between operations  15 us (8%)
  other arithmetic  12.3 us (6%)
  local copies, waits for them, and re-layouts  2.06 us (1%)
    ppermute x16, waiting for transfers between devices, shifted(): lax.ppermute(array, axis, [(i, (i + by) % length) for i in range(length)])  57.8 us
    ppermute x14, starting transfers between devices, passed_along(): return lax.ppermute(array, axis, pairs)  44.5 us
    psum x1, blocking collectives, body(): key_sum, value_sum = lax.psum((key_acc, value_acc), 'hd')  16.3 us
    dot_general x7, matrix products, stat_block(): jnp.einsum('thd,kd->htk', grad_heads, value_block, preferred_element_type...  11.3 us
    psum x1, waiting for transfers between devices, body(): key_sum, value_sum = lax.psum((key_acc, value_acc), 'hd')  7.56 us
    convert_element_type x2, other arithmetic, grad_block(): (probs * (grad_prob - row_delta[..., None])).astype(jnp.bfloat16)  7.54 us
    dot_general x8, matrix products, grad_block(): jnp.einsum('htk,thd->kd', grad_score, query_heads, preferred_element_type...  5.13 us
    dot_general x8, matrix products, grad_block(): jnp.einsum('htk,thd->kd', probs_low, grad_heads, preferred_element_type=j...  4.99 us
  transfers between devices with their start and end apart: 31, of which 16 were waited for; matrix products, arithmetic and copies ran while one was open for 18% of the time, Pallas kernels for 0%

commit v1 on v0

v1 whole, which is shorter than its diff:
```python
import functools
import math

import jax
import jax.numpy as jnp
from jax import lax
from jax.experimental import pallas as pl
from jax.experimental.pallas import tpu as pltpu
from jax.sharding import PartitionSpec as P

HDIM = 128
MAXDOC = 4096
MESH = pl.DeviceIdType.MESH
BF16 = jnp.bfloat16
F32 = jnp.float32
MASKED = -1e30


def xor3(a, b):
    out = 0
    for bit in (1, 2, 4):
        x, y = (a // bit) % 2, (b // bit) % 2
        out = out + bit * (x + y - 2 * x * y)
    return out


def dot(a, b, contract=((1,), (0,))):
    return lax.dot_general(a, b, (contract, ((), ())), preferred_element_type=F32)


def kernel(
    span,
    q_ref, k_ref, v_ref, do_ref, start_ref,
    dq_ref, dk_ref, dv_ref,
    kv, qs, dos, qt, dot_t, e_all, d_all, m_all, m_run, l_run, w_run, dq_t, acc,
    sib_out, sib_in, red_out, red_in, hd_out, hd_in,
    kv_send, kv_recv, sib_send, sib_recv, red_send, red_recv, hd_sem,
):
    rows = k_ref.shape[0]
    heads = q_ref.shape[1] // HDIM
    wide = heads * rows
    chunk = rows // 2
    tile = rows // 2
    scaling = 1.0 / math.sqrt(HDIM)
    scale2 = scaling * math.log2(math.e)

    pos = lax.axis_index("cp")
    me = pos % span
    base = pos - me
    twin = {"hd": 1 - lax.axis_index("hd")}

    def peer(index):
        return {"cp": base + index}

    sibling = xor3(me, 1)
    partners = [xor3(me, 2 * d) for d in range(1, span // 2)]

    barrier = pltpu.get_barrier_semaphore()
    for other in [peer(sibling)] + [peer(p) for p in partners] + [twin]:
        pl.semaphore_signal(barrier, inc=1, device_id=other, device_id_type=MESH)
    pl.semaphore_wait(barrier, 2 + len(partners))

    def remote(src, dst, send, recv, device):
        return pltpu.make_async_remote_copy(
            src_ref=src, dst_ref=dst, send_sem=send, recv_sem=recv,
            device_id=device, device_id_type=MESH,
        )

    def own_copy(d, target):
        return remote(kv.at[me], kv.at[me], kv_send.at[d], kv_recv.at[me], peer(target))

    def relay_copy(d, slot):
        return remote(
            kv.at[slot], kv.at[slot], kv_send.at[span // 2 + d], kv_recv.at[slot], peer(sibling)
        )

    def sib_copy(d):
        return remote(
            sib_out.at[d], sib_in.at[d], sib_send.at[d], sib_recv.at[d], peer(sibling)
        )

    def red_copy(d, target):
        return remote(
            red_out.at[d], red_in.at[d], red_send.at[d], red_recv.at[d], peer(target)
        )

    kv[me, 0] = k_ref[...]
    kv[me, 1] = v_ref[...]
    for d, target in enumerate(partners, 1):
        @pl.when(target > me)
        def _():
            own_copy(d, target).start()

    @pl.when(sibling > me)
    def _():
        own_copy(0, sibling).start()

    for h in range(heads):
        at = slice(h * rows, (h + 1) * rows)
        q = q_ref[:, h * HDIM:(h + 1) * HDIM]
        g = do_ref[:, h * HDIM:(h + 1) * HDIM]
        qs[at, :] = q
        dos[at, :] = g
        qt[:, at] = q.T
        dot_t[:, at] = g.T
    m_run[...] = jnp.full_like(m_run, MASKED)
    l_run[...] = jnp.zeros_like(l_run)
    w_run[...] = jnp.zeros_like(w_run)
    dq_t[...] = jnp.zeros_like(dq_t)

    def stat_tile(s, kc, tq, diagonal):
        at_k = slice(kc * chunk, (kc + 1) * chunk)
        at_q = slice(tq * tile, (tq + 1) * tile)
        row0 = (tq * tile) % rows
        scores = dot(kv[s, 0, at_k, :], qt[:, at_q]) * scale2
        grad_prob = dot(kv[s, 1, at_k, :], dot_t[:, at_q])
        key_pos = lax.broadcasted_iota(jnp.int32, (chunk, tile), 0)
        first = start_ref[:, row0:row0 + tile] - ((base + s) * rows + kc * chunk)
        allowed = key_pos >= first
        if diagonal:
            query_pos = lax.broadcasted_iota(jnp.int32, (chunk, tile), 1) + (row0 - kc * chunk)
            allowed = allowed & (key_pos <= query_pos)
        scores = jnp.where(allowed, scores, MASKED)
        old = m_run[:, at_q]
        new = jnp.maximum(old, jnp.max(scores, axis=0, keepdims=True))
        e = jnp.exp2(scores - new)
        fac = jnp.exp2(old - new)
        l_run[:, at_q] = l_run[:, at_q] * fac + jnp.sum(e, axis=0, keepdims=True)
        w_run[:, at_q] = w_run[:, at_q] * fac + jnp.sum(e * grad_prob, axis=0, keepdims=True)
        m_run[:, at_q] = new
        m_all[s, kc, :, at_q] = new
        e_all[s, at_k, at_q] = e
        d_all[s, at_k, at_q] = grad_prob

    for tq in range(wide // tile):
        first_kc = tq % (rows // tile)
        for kc in (first_kc, 1 - first_kc):
            stat_tile(me, kc, tq, True)

    def stat_step(t, _):
        s = xor3(me, t)

        @pl.when(s < me)
        def _():
            relay_copy(0, s).wait_recv()

            @pl.when(t % 2 == 0)
            def _():
                relay_copy(t // 2, s).start()

            for tq in range(wide // tile):
                for kc in range(rows // chunk):
                    stat_tile(s, kc, tq, False)

        return 0

    lax.fori_loop(1, span, stat_step, 0)

    inv = 1.0 / l_run[...]
    l_run[...] = inv
    w_run[...] = w_run[...] * inv

    def grad_step(i, _):
        t = span - 1 - i
        s = xor3(me, t)
        d = t // 2

        @pl.when(s <= me)
        def _():
            delta = w_run[...]
            for kc in range(rows // chunk):
                at_k = slice(kc * chunk, (kc + 1) * chunk)
                fac = jnp.exp2(m_all[s, kc] - m_run[...]) * l_run[...]
                p = e_all[s, at_k, :] * fac
                ds = (p * (d_all[s, at_k, :] - delta)).astype(BF16)
                acc[0, at_k, :] = dot(ds, qs[...])
                acc[1, at_k, :] = dot(p.astype(BF16), dos[...])
                dq_t[...] += dot(kv[s, 0, at_k, :], ds, ((0,), (0,)))

            @pl.when(t % 2 == 1)
            def _():
                sib_out[d] = acc[...].astype(BF16)
                sib_copy(d).start()

            @pl.when((t % 2 == 0) & (t > 0))
            def _():
                sib_copy(d).wait_recv()
                red_out[d] = (acc[...] + sib_in[d].astype(F32)).astype(BF16)
                red_copy(d, s).start()

        return 0

    lax.fori_loop(0, span, grad_step, 0)

    for h in range(heads):
        dq_ref[:, h * HDIM:(h + 1) * HDIM] = (
            (dq_t[:, h * rows:(h + 1) * rows] * scaling).T.astype(BF16)
        )

    @pl.when(sibling > me)
    def _():
        sib_copy(0).wait_recv()
        acc[...] += sib_in[0].astype(F32)

    for d, target in enumerate(partners, 1):
        @pl.when(target > me)
        def _():
            red_copy(d, target).wait_recv()
            acc[...] += red_in[d].astype(F32)

    hd_out[...] = acc[...].astype(BF16)
    hd_copy = remote(hd_out, hd_in, hd_sem.at[0], hd_sem.at[1], twin)
    hd_copy.start()
    hd_copy.wait()
    dk_ref[...] = ((hd_out[0].astype(F32) + hd_in[0].astype(F32)) * scaling).astype(BF16)
    dv_ref[...] = (hd_out[1].astype(F32) + hd_in[1].astype(F32)).astype(BF16)

    @pl.when(sibling > me)
    def _():
        own_copy(0, sibling).wait_send()

    @pl.when(sibling < me)
    def _():
        sib_copy(0).wait_send()

    for d, target in enumerate(partners, 1):
        @pl.when(target > me)
        def _():
            own_copy(d, target).wait_send()

        @pl.when(target < me)
        def _():
            relay_copy(d, target).wait_send()
            sib_copy(d).wait_send()
            red_copy(d, target).wait_send()


def body(query, keys, values, grad_out, doc_start):
    rows = keys.shape[0]
    heads = query.shape[1] // HDIM
    wide = heads * rows
    span = MAXDOC // rows
    vmem = pl.BlockSpec(memory_space=pltpu.VMEM)
    pair = (2, rows, HDIM)
    return pl.pallas_call(
        functools.partial(kernel, span),
        out_shape=(
            jax.ShapeDtypeStruct(query.shape, BF16),
            jax.ShapeDtypeStruct(keys.shape, BF16),
            jax.ShapeDtypeStruct(values.shape, BF16),
        ),
        in_specs=[vmem] * 5,
        out_specs=(vmem,) * 3,
        scratch_shapes=[
            pltpu.VMEM((span,) + pair, BF16),
            pltpu.VMEM((wide, HDIM), BF16),
            pltpu.VMEM((wide, HDIM), BF16),
            pltpu.VMEM((HDIM, wide), BF16),
            pltpu.VMEM((HDIM, wide), BF16),
            pltpu.VMEM((span, rows, wide), F32),
            pltpu.VMEM((span, rows, wide), F32),
            pltpu.VMEM((span, 2, 1, wide), F32),
            pltpu.VMEM((1, wide), F32),
            pltpu.VMEM((1, wide), F32),
            pltpu.VMEM((1, wide), F32),
            pltpu.VMEM((HDIM, wide), F32),
            pltpu.VMEM(pair, F32),
            pltpu.VMEM((span // 2,) + pair, BF16),
            pltpu.VMEM((span // 2,) + pair, BF16),
            pltpu.VMEM((span // 2,) + pair, BF16),
            pltpu.VMEM((span // 2,) + pair, BF16),
            pltpu.VMEM(pair, BF16),
            pltpu.VMEM(pair, BF16),
            pltpu.SemaphoreType.DMA((span,)),
            pltpu.SemaphoreType.DMA((span,)),
            pltpu.SemaphoreType.DMA((span // 2,)),
            pltpu.SemaphoreType.DMA((span // 2,)),
            pltpu.SemaphoreType.DMA((span // 2,)),
            pltpu.SemaphoreType.DMA((span // 2,)),
            pltpu.SemaphoreType.DMA((2,)),
        ],
        compiler_params=pltpu.CompilerParams(
            collective_id=0, has_side_effects=True, vmem_limit_bytes=56 * 1024 * 1024
        ),
    )(query, keys, values, grad_out, doc_start.reshape(1, rows))


def solution(mesh):
    in_specs = (P("cp", "hd"), P("cp", None), P("cp", None), P("cp", "hd"), P("cp"))
    out_specs = (P("cp", "hd"), P("cp", None), P("cp", None))
    return jax.shard_map(body, mesh=mesh, in_specs=in_specs, out_specs=out_specs, check_vma=False)
```

time: 190 us -> 48.5 us (0.26)
  waiting for transfers between devices: 65.4 us -> 0 us
  starting transfers between devices: 48.9 us -> 0 us
  Pallas kernels: 0 us -> 44.3 us
  matrix products: 29.5 us -> 0 us
  blocking collectives: 16.3 us -> 0 us
  between operations: 15 us -> 0.65 us
  other arithmetic: 12.3 us -> 0 us
    ppermute x30 -> x0, waiting for transfers between devices: 57.8 us -> none  [the longest x16 57.8 us: shifted(): lax.ppermute(array, axis, [(i, (i + by) % length) for i in range(length)])]
    ppermute x30 -> x0, starting transfers between devices: 48.8 us -> none  [the longest x14 44.5 us: passed_along(): return lax.ppermute(array, axis, pairs)]
    pallas_call x0 -> x1, Pallas kernels: none -> 44.3 us  [body(): pl.pallas_call(functools.partial(kernel, span), out_shape=(jax.ShapeDtype...]
    dot_general x40 -> x0, matrix products: 29.5 us -> none  [the longest x7 11.3 us: stat_block(): jnp.einsum('thd,kd->htk', grad_heads, value_block, preferred_element_type...]
    psum x1 -> x0, blocking collectives: 16.3 us -> none  [body(): key_sum, value_sum = lax.psum((key_acc, value_acc), 'hd')]
    convert_element_type x3 -> x0, other arithmetic: 9.16 us -> none  [the longest x2 7.54 us: grad_block(): (probs * (grad_prob - row_delta[..., None])).astype(jnp.bfloat16)]
    psum x1 -> x0, waiting for transfers between devices: 7.56 us -> none  [body(): key_sum, value_sum = lax.psum((key_acc, value_acc), 'hd')]
    and x1 -> x0, other arithmetic: 2.67 us -> none  [key_mask(): (key_pos[None, :] >= start_rows[:, None]) & (key_pos[None, :] <= query_po...]
  transfers between devices with their start and end apart: 31 -> 0, of which waited for: 16 -> 0; matrix products, arithmetic and copies ran while one was open for 18% -> 0% of each run, Pallas kernels for 0% -> 0%
where the time goes in v1:
time: 48.5 us; the launch traced here: 48.3 us
  Pallas kernels  44.3 us (91%)
  local copies, waits for them, and re-layouts  3.31 us (7%)
  between operations  0.65 us (1%)
    pallas_call x1, Pallas kernels, body(): pl.pallas_call(functools.partial(kernel, span), out_shape=(jax.ShapeDtype...  44.3 us
    unnamed x7, local copies, waits for them, and re-layouts  3.31 us

profile of v1, /device:TPU:0, one launch (start us, length us, event | category | flops | bytes accessed | tf_op | source)
XLA Modules:
  0.0 48.3 jit_solution(17463005345734042278)
XLA Ops:
  0.6 44.3 %shard_map.76 = (bf16[512,256]{1,0:T(8,128)(2,1)}, bf16[512,128]{1,0:T(8,128)(2,1)}, bf16[512,128]{1,0:T(8,128)(2,1)}) custom-call(bf16[512,256]{1,0:T(8,128)(2,1)} %q_ref.1, bf16[512,128]{1,0:T(8,128)(2,1)} %k_ref.1, bf16[512,128]{1,0:T(8,128)(2,1)} %v_ref.1, bf16[512,256]{1,0:T(8,128)(2,1)} %do_ref.1, s32[1,512]{1,0:T(1,128)} %bitcast.1), custom_call_target="tpu_custom_call" | custom-call | tf_op jit(solution)/shard_map/pallas_call | solution.py:245
  45.0 0.0 copy-start.1
  45.0 1.7 %copy.11 = bf16[512,256]{1,0:T(8,128)(2,1)} copy(bf16[512,256]{1,0:T(8,128)(2,1)} %get-tuple-element.6) | data formatting | bytes 524288
  46.7 0.0 copy-done.1
  46.7 0.0 copy-start
  46.7 0.7 %copy.12 = bf16[512,128]{1,0:T(8,128)(2,1)} copy(bf16[512,128]{1,0:T(8,128)(2,1)S(1)} %copy-done.1) | data formatting | bytes 262144
  47.4 0.3 copy-done
  47.6 0.7 %copy.13 = bf16[512,128]{1,0:T(8,128)(2,1)} copy(bf16[512,128]{1,0:T(8,128)(2,1)S(1)} %copy-done) | data formatting | bytes 262144
Async XLA Ops:
  45.0 1.7 %copy-start.1 = (bf16[512,128]{1,0:T(8,128)(2,1)S(1)}, bf16[512,128]{1,0:T(8,128)(2,1)}, u32[]{:S(2)}) copy-start(bf16[512,128]{1,0:T(8,128)(2,1)} %get-tuple-element.7) | copy-start | bytes 393220
  46.7 1.0 %copy-start = (bf16[512,128]{1,0:T(8,128)(2,1)S(1)}, bf16[512,128]{1,0:T(8,128)(2,1)}, u32[]{:S(2)}) copy-start(bf16[512,128]{1,0:T(8,128)(2,1)} %get-tuple-element.8) | copy-start | bytes 393220

commit v2 on v1

--- a/solution.py
+++ b/solution.py
@@ -47,18 +47,19 @@
     pos = lax.axis_index("cp")
     me = pos % span
     base = pos - me
-    twin = {"hd": 1 - lax.axis_index("hd")}
-
-    def peer(index):
-        return {"cp": base + index}
+    side = lax.axis_index("hd")
+    twin = {"hd": 1 - side}
+
+    def peer(index, hd=None):
+        return {"cp": base + index} if hd is None else {"cp": base + index, "hd": hd}
 
     sibling = xor3(me, 1)
     partners = [xor3(me, 2 * d) for d in range(1, span // 2)]
 
     barrier = pltpu.get_barrier_semaphore()
-    for other in [peer(sibling)] + [peer(p) for p in partners] + [twin]:
+    for other in [peer(sibling), twin] + [peer(p, hd) for p in partners for hd in (0, 1)]:
         pl.semaphore_signal(barrier, inc=1, device_id=other, device_id_type=MESH)
-    pl.semaphore_wait(barrier, 2 + len(partners))
+    pl.semaphore_wait(barrier, 2 + 2 * len(partners))
 
     def remote(src, dst, send, recv, device):
         return pltpu.make_async_remote_copy(
@@ -79,9 +80,16 @@
             sib_out.at[d], sib_in.at[d], sib_send.at[d], sib_recv.at[d], peer(sibling)
         )
 
-    def red_copy(d, target):
+    def red_copy(d, part, target):
         return remote(
-            red_out.at[d], red_in.at[d], red_send.at[d], red_recv.at[d], peer(target)
+            red_out.at[d, part], red_in.at[d, side], red_send.at[d, part],
+            red_recv.at[d, side], peer(target, part),
+        )
+
+    def red_arrival(d, source):
+        return remote(
+            red_out.at[d, 0], red_in.at[d, source], red_send.at[d, 0],
+            red_recv.at[d, source], twin,
         )
 
     kv[me, 0] = k_ref[...]
@@ -186,34 +194,51 @@
             def _():
                 sib_copy(d).wait_recv()
                 red_out[d] = (acc[...] + sib_in[d].astype(F32)).astype(BF16)
-                red_copy(d, s).start()
+                for part in (0, 1):
+                    red_copy(d, part, s).start()
 
         return 0
 
     lax.fori_loop(0, span, grad_step, 0)
+
+    @pl.when(sibling > me)
+    def _():
+        sib_copy(0).wait_recv()
+        acc[...] += sib_in[0].astype(F32)
+
+    hd_out[0] = acc[1 - side].astype(BF16)
+    swap = remote(hd_out.at[0], hd_in.at[0], hd_sem.at[0], hd_sem.at[1], twin)
+    swap.start()
 
     for h in range(heads):
         dq_ref[:, h * HDIM:(h + 1) * HDIM] = (
             (dq_t[:, h * rows:(h + 1) * rows] * scaling).T.astype(BF16)
         )
 
-    @pl.when(sibling > me)
-    def _():
-        sib_copy(0).wait_recv()
-        acc[...] += sib_in[0].astype(F32)
+    swap.wait()
+    acc[side] += hd_in[0].astype(F32)
 
     for d, target in enumerate(partners, 1):
         @pl.when(target > me)
         def _():
-            red_copy(d, target).wait_recv()
-            acc[...] += red_in[d].astype(F32)
-
-    hd_out[...] = acc[...].astype(BF16)
-    hd_copy = remote(hd_out, hd_in, hd_sem.at[0], hd_sem.at[1], twin)
-    hd_copy.start()
-    hd_copy.wait()
-    dk_ref[...] = ((hd_out[0].astype(F32) + hd_in[0].astype(F32)) * scaling).astype(BF16)
-    dv_ref[...] = (hd_out[1].astype(F32) + hd_in[1].astype(F32)).astype(BF16)
+            for source in (0, 1):
+                red_arrival(d, source).wait_recv()
+                acc[side] += red_in[d, source].astype(F32)
+
+    hd_out[1] = (acc[side] * jnp.where(side == 0, scaling, 1.0)).astype(BF16)
+    finished = remote(hd_out.at[1], hd_in.at[1], hd_sem.at[2], hd_sem.at[3], twin)
+    finished.start()
+    finished.wait()
+
+    @pl.when(side == 0)
+    def _():
+        dk_ref[...] = hd_out[1]
+        dv_ref[...] = hd_in[1]
+
+    @pl.when(side != 0)
+    def _():
+        dk_ref[...] = hd_in[1]
+        dv_ref[...] = hd_out[1]
 
     @pl.when(sibling > me)
     def _():
@@ -232,7 +257,19 @@
         def _():
             relay_copy(d, target).wait_send()
             sib_copy(d).wait_send()
-            red_copy(d, target).wait_send()
+            for part in (0, 1):
+                red_copy(d, part, target).wait_send()
+
+
+def copy_out(a, b, c, out_a, out_b, out_c, sems):
+    copies = [
+        pltpu.make_async_copy(src, dst, sems.at[i])
+        for i, (src, dst) in enumerate(((a, out_a), (b, out_b), (c, out_c)))
+    ]
+    for copy in copies:
+        copy.start()
+    for copy in copies:
+        copy.wait()
 
 
 def body(query, keys, values, grad_out, doc_start):
@@ -242,7 +279,7 @@
     span = MAXDOC // rows
     vmem = pl.BlockSpec(memory_space=pltpu.VMEM)
     pair = (2, rows, HDIM)
-    return pl.pallas_call(
+    grads = pl.pallas_call(
         functools.partial(kernel, span),
         out_shape=(
             jax.ShapeDtypeStruct(query.shape, BF16),
@@ -275,14 +312,23 @@
             pltpu.SemaphoreType.DMA((span,)),
             pltpu.SemaphoreType.DMA((span // 2,)),
             pltpu.SemaphoreType.DMA((span // 2,)),
-            pltpu.SemaphoreType.DMA((span // 2,)),
-            pltpu.SemaphoreType.DMA((span // 2,)),
-            pltpu.SemaphoreType.DMA((2,)),
+            pltpu.SemaphoreType.DMA((span // 2, 2)),
+            pltpu.SemaphoreType.DMA((span // 2, 2)),
+            pltpu.SemaphoreType.DMA((4,)),
         ],
         compiler_params=pltpu.CompilerParams(
             collective_id=0, has_side_effects=True, vmem_limit_bytes=56 * 1024 * 1024
         ),
     )(query, keys, values, grad_out, doc_start.reshape(1, rows))
+    anywhere = pl.BlockSpec(memory_space=pl.ANY)
+    return pl.pallas_call(
+        copy_out,
+        out_shape=tuple(jax.ShapeDtypeStruct(g.shape, g.dtype) for g in grads),
+        in_specs=[anywhere] * 3,
+        out_specs=(anywhere,) * 3,
+        scratch_shapes=[pltpu.SemaphoreType.DMA((3,))],
+        compiler_params=pltpu.CompilerParams(vmem_limit_bytes=60 * 1024 * 1024),
+    )(*grads)
 
 
 def solution(mesh):

time: 48.5 us -> 60.3 us (1.24)
  Pallas kernels: 44.3 us -> 59.5 us
  local copies, waits for them, and re-layouts: 3.31 us -> 0 us
    pallas_call x0 -> x1, Pallas kernels: none -> 17 us  [body(): pl.pallas_call(copy_out, out_shape=tuple((jax.ShapeDtypeStruct(g.shape, g...]
    unnamed x7 -> x0, local copies, waits for them, and re-layouts: 3.31 us -> none
    pallas_call x1, Pallas kernels: 44.3 us -> 42.5 us  [body(): pl.pallas_call(functools.partial(kernel, span), out_shape=(jax.ShapeDtype...]
where the time goes in v2:
time: 60.3 us; the launch traced here: 60.1 us
  Pallas kernels  59.5 us (99%)
  between operations  0.64 us (1%)
    pallas_call x1, Pallas kernels, body(): pl.pallas_call(functools.partial(kernel, span), out_shape=(jax.ShapeDtype...  42.5 us
    pallas_call x1, Pallas kernels, body(): pl.pallas_call(copy_out, out_shape=tuple((jax.ShapeDtypeStruct(g.shape, g...  17 us

profile of v2, /device:TPU:0, one launch (start us, length us, event | category | flops | bytes accessed | tf_op | source)
XLA Modules:
  0.0 60.1 jit_solution(11042749822017023326)
XLA Ops:
  0.6 42.5 %shard_map.76 = (bf16[512,256]{1,0:T(8,128)(2,1)}, bf16[512,128]{1,0:T(8,128)(2,1)}, bf16[512,128]{1,0:T(8,128)(2,1)}) custom-call(bf16[512,256]{1,0:T(8,128)(2,1)} %q_ref.1, bf16[512,128]{1,0:T(8,128)(2,1)} %k_ref.1, bf16[512,128]{1,0:T(8,128)(2,1)} %v_ref.1, bf16[512,256]{1,0:T(8,128)(2,1)} %do_ref.1, s32[1,512]{1,0:T(1,128)} %bitcast.1), custom_call_target="tpu_custom_call" | custom-call | tf_op jit(solution)/shard_map/pallas_call | solution.py:282
  43.1 17.0 %shard_map.77 = (bf16[512,256]{1,0:T(8,128)(2,1)}, bf16[512,128]{1,0:T(8,128)(2,1)}, bf16[512,128]{1,0:T(8,128)(2,1)}) custom-call(bf16[512,256]{1,0:T(8,128)(2,1)} %get-tuple-element.6.a, bf16[512,128]{1,0:T(8,128)(2,1)} %get-tuple-element.7.b, bf16[512,128]{1,0:T(8,128)(2,1)} %get-tuple-element.8.c), custom_call_target="tpu_custom_call" | custom-call | tf_op jit(solution)/shard_map/pallas_call | solution.py:324

commit v3 on v2

--- a/solution.py
+++ b/solution.py
@@ -32,7 +32,7 @@
     span,
     q_ref, k_ref, v_ref, do_ref, start_ref,
     dq_ref, dk_ref, dv_ref,
-    kv, qs, dos, qt, dot_t, e_all, d_all, m_all, m_run, l_run, w_run, dq_t, acc,
+    kv, qs, dos, qt, dot_t, e_all, d_all, raw0, raw1, p0, p1, ds0, ds1, m_run, l_run, w_run, dq_t, acc,
     sib_out, sib_in, red_out, red_in, hd_out, hd_in,
     kv_send, kv_recv, sib_send, sib_recv, red_send, red_recv, hd_sem,
 ):
@@ -41,6 +41,8 @@
     wide = heads * rows
     chunk = rows // 2
     tile = rows // 2
+    piece = 32
+    raw, p_halves, ds_halves = (raw0, raw1), (p0, p1), (ds0, ds1)
     scaling = 1.0 / math.sqrt(HDIM)
     scale2 = scaling * math.log2(math.e)
 
@@ -116,34 +118,51 @@
     w_run[...] = jnp.zeros_like(w_run)
     dq_t[...] = jnp.zeros_like(dq_t)
 
-    def stat_tile(s, kc, tq, diagonal):
-        at_k = slice(kc * chunk, (kc + 1) * chunk)
+    def load_tile(s, tq):
+        at_q = slice(tq * tile, (tq + 1) * tile)
+        raw[tq % 2][...] = dot(kv[s, 0], qt[:, at_q])
+        d_all[s, :, at_q] = dot(kv[s, 1], dot_t[:, at_q])
+
+    def stat_tile(s, tq, diagonal):
         at_q = slice(tq * tile, (tq + 1) * tile)
         row0 = (tq * tile) % rows
-        scores = dot(kv[s, 0, at_k, :], qt[:, at_q]) * scale2
-        grad_prob = dot(kv[s, 1, at_k, :], dot_t[:, at_q])
-        key_pos = lax.broadcasted_iota(jnp.int32, (chunk, tile), 0)
-        first = start_ref[:, row0:row0 + tile] - ((base + s) * rows + kc * chunk)
-        allowed = key_pos >= first
+        source = raw[tq % 2]
+        first = start_ref[:, row0:row0 + tile] - (base + s) * rows
+        key_pos = lax.broadcasted_iota(jnp.int32, (piece, tile), 0)
         if diagonal:
-            query_pos = lax.broadcasted_iota(jnp.int32, (chunk, tile), 1) + (row0 - kc * chunk)
-            allowed = allowed & (key_pos <= query_pos)
-        scores = jnp.where(allowed, scores, MASKED)
+            query_pos = lax.broadcasted_iota(jnp.int32, (piece, tile), 1) + row0
         old = m_run[:, at_q]
-        new = jnp.maximum(old, jnp.max(scores, axis=0, keepdims=True))
-        e = jnp.exp2(scores - new)
+        top = jnp.broadcast_to(old, (8, tile))
+        for r in range(0, rows, piece):
+            at_k = slice(r, r + piece)
+            allowed = key_pos >= first - r
+            if diagonal:
+                allowed = allowed & (key_pos + r <= query_pos)
+            scores = jnp.where(allowed, source[at_k, :] * scale2, MASKED)
+            e_all[s, at_k, at_q] = scores
+            top = jnp.maximum(top, jnp.max(scores.reshape(piece // 8, 8, tile), axis=0))
+        new = jnp.max(top, axis=0, keepdims=True)
+        total = jnp.zeros((8, tile), F32)
+        weighted = jnp.zeros((8, tile), F32)
+        for r in range(0, rows, piece):
+            at_k = slice(r, r + piece)
+            e = jnp.exp2(e_all[s, at_k, at_q] - new)
+            ed = e * d_all[s, at_k, at_q]
+            total = total + jnp.sum(e.reshape(piece // 8, 8, tile), axis=0)
+            weighted = weighted + jnp.sum(ed.reshape(piece // 8, 8, tile), axis=0)
         fac = jnp.exp2(old - new)
-        l_run[:, at_q] = l_run[:, at_q] * fac + jnp.sum(e, axis=0, keepdims=True)
-        w_run[:, at_q] = w_run[:, at_q] * fac + jnp.sum(e * grad_prob, axis=0, keepdims=True)
+        l_run[:, at_q] = l_run[:, at_q] * fac + jnp.sum(total, axis=0, keepdims=True)
+        w_run[:, at_q] = w_run[:, at_q] * fac + jnp.sum(weighted, axis=0, keepdims=True)
         m_run[:, at_q] = new
-        m_all[s, kc, :, at_q] = new
-        e_all[s, at_k, at_q] = e
-        d_all[s, at_k, at_q] = grad_prob
-
-    for tq in range(wide // tile):
-        first_kc = tq % (rows // tile)
-        for kc in (first_kc, 1 - first_kc):
-            stat_tile(me, kc, tq, True)
+
+    def stat_block(s, diagonal):
+        load_tile(s, 0)
+        for tq in range(wide // tile):
+            if tq + 1 < wide // tile:
+                load_tile(s, tq + 1)
+            stat_tile(s, tq, diagonal)
+
+    stat_block(me, True)
 
     def stat_step(t, _):
         s = xor3(me, t)
@@ -156,17 +175,14 @@
             def _():
                 relay_copy(t // 2, s).start()
 
-            for tq in range(wide // tile):
-                for kc in range(rows // chunk):
-                    stat_tile(s, kc, tq, False)
+            stat_block(s, False)
 
         return 0
 
     lax.fori_loop(1, span, stat_step, 0)
 
-    inv = 1.0 / l_run[...]
-    l_run[...] = inv
-    w_run[...] = w_run[...] * inv
+    w_run[...] = w_run[...] / l_run[...]
+    m_run[...] = m_run[...] + jnp.log2(l_run[...])
 
     def grad_step(i, _):
         t = span - 1 - i
@@ -175,15 +191,24 @@
 
         @pl.when(s <= me)
         def _():
-            delta = w_run[...]
+            dq_term = None
             for kc in range(rows // chunk):
+                p_low, ds_low = p_halves[kc], ds_halves[kc]
+                for tq in range(wide // tile):
+                    at_q = slice(tq * tile, (tq + 1) * tile)
+                    norm, delta = m_run[:, at_q], w_run[:, at_q]
+                    for r in range(0, chunk, piece):
+                        at_k = slice(kc * chunk + r, kc * chunk + r + piece)
+                        p = jnp.exp2(e_all[s, at_k, at_q] - norm)
+                        ds = p * (d_all[s, at_k, at_q] - delta)
+                        p_low[r:r + piece, at_q] = p.astype(BF16)
+                        ds_low[r:r + piece, at_q] = ds.astype(BF16)
                 at_k = slice(kc * chunk, (kc + 1) * chunk)
-                fac = jnp.exp2(m_all[s, kc] - m_run[...]) * l_run[...]
-                p = e_all[s, at_k, :] * fac
-                ds = (p * (d_all[s, at_k, :] - delta)).astype(BF16)
-                acc[0, at_k, :] = dot(ds, qs[...])
-                acc[1, at_k, :] = dot(p.astype(BF16), dos[...])
-                dq_t[...] += dot(kv[s, 0, at_k, :], ds, ((0,), (0,)))
+                acc[0, at_k, :] = dot(ds_low[...], qs[...])
+                acc[1, at_k, :] = dot(p_low[...], dos[...])
+                term = dot(kv[s, 0, at_k, :], ds_low[...], ((0,), (0,)))
+                dq_term = term if dq_term is None else dq_term + term
+            dq_t[...] += dq_term
 
             @pl.when(t % 2 == 1)
             def _():
@@ -261,15 +286,10 @@
                 red_copy(d, part, target).wait_send()
 
 
-def copy_out(a, b, c, out_a, out_b, out_c, sems):
-    copies = [
-        pltpu.make_async_copy(src, dst, sems.at[i])
-        for i, (src, dst) in enumerate(((a, out_a), (b, out_b), (c, out_c)))
-    ]
-    for copy in copies:
-        copy.start()
-    for copy in copies:
-        copy.wait()
+def copy_out(a, b, c, out_a, out_b, out_c):
+    out_a[...] = a[...]
+    out_b[...] = b[...]
+    out_c[...] = c[...]
 
 
 def body(query, keys, values, grad_out, doc_start):
@@ -296,7 +316,12 @@
             pltpu.VMEM((HDIM, wide), BF16),
             pltpu.VMEM((span, rows, wide), F32),
             pltpu.VMEM((span, rows, wide), F32),
-            pltpu.VMEM((span, 2, 1, wide), F32),
+            pltpu.VMEM((rows, rows // 2), F32),
+            pltpu.VMEM((rows, rows // 2), F32),
+            pltpu.VMEM((rows // 2, wide), BF16),
+            pltpu.VMEM((rows // 2, wide), BF16),
+            pltpu.VMEM((rows // 2, wide), BF16),
+            pltpu.VMEM((rows // 2, wide), BF16),
             pltpu.VMEM((1, wide), F32),
             pltpu.VMEM((1, wide), F32),
             pltpu.VMEM((1, wide), F32),
@@ -320,13 +345,11 @@
             collective_id=0, has_side_effects=True, vmem_limit_bytes=56 * 1024 * 1024
         ),
     )(query, keys, values, grad_out, doc_start.reshape(1, rows))
-    anywhere = pl.BlockSpec(memory_space=pl.ANY)
     return pl.pallas_call(
         copy_out,
         out_shape=tuple(jax.ShapeDtypeStruct(g.shape, g.dtype) for g in grads),
-        in_specs=[anywhere] * 3,
-        out_specs=(anywhere,) * 3,
-        scratch_shapes=[pltpu.SemaphoreType.DMA((3,))],
+        in_specs=[vmem] * 3,
+        out_specs=(vmem,) * 3,
         compiler_params=pltpu.CompilerParams(vmem_limit_bytes=60 * 1024 * 1024),
     )(*grads)
 

time: 60.3 us -> 45.5 us (0.75)
  Pallas kernels: 59.5 us -> 44.7 us
    pallas_call x1, Pallas kernels: 17 us -> 1.84 us  [body(): pl.pallas_call(copy_out, out_shape=tuple((jax.ShapeDtypeStruct(g.shape, g...]
where the time goes in v3:
time: 45.5 us; the launch traced here: 45.4 us
  Pallas kernels  44.7 us (98%)
  between operations  0.64 us (1%)
    pallas_call x1, Pallas kernels, body(): pl.pallas_call(functools.partial(kernel, span), out_shape=(jax.ShapeDtype...  42.9 us
    pallas_call x1, Pallas kernels, body(): pl.pallas_call(copy_out, out_shape=tuple((jax.ShapeDtypeStruct(g.shape, g...  1.84 us

profile of v3, /device:TPU:0, one launch (start us, length us, event | category | flops | bytes accessed | tf_op | source)
XLA Modules:
  0.0 45.4 jit_solution(5262576970610438315)
XLA Ops:
  0.6 42.9 %shard_map.76 = (bf16[512,256]{1,0:T(8,128)(2,1)}, bf16[512,128]{1,0:T(8,128)(2,1)}, bf16[512,128]{1,0:T(8,128)(2,1)}) custom-call(bf16[512,256]{1,0:T(8,128)(2,1)} %q_ref.1, bf16[512,128]{1,0:T(8,128)(2,1)} %k_ref.1, bf16[512,128]{1,0:T(8,128)(2,1)} %v_ref.1, bf16[512,256]{1,0:T(8,128)(2,1)} %do_ref.1, s32[1,512]{1,0:T(1,128)} %bitcast.1), custom_call_target="tpu_custom_call" | custom-call | tf_op jit(solution)/shard_map/pallas_call | solution.py:302
  43.5 1.8 %shard_map.77 = (bf16[512,256]{1,0:T(8,128)(2,1)}, bf16[512,128]{1,0:T(8,128)(2,1)}, bf16[512,128]{1,0:T(8,128)(2,1)}) custom-call(bf16[512,256]{1,0:T(8,128)(2,1)} %get-tuple-element.6.a, bf16[512,128]{1,0:T(8,128)(2,1)} %get-tuple-element.7.b, bf16[512,128]{1,0:T(8,128)(2,1)} %get-tuple-element.8.c), custom_call_target="tpu_custom_call" | custom-call | tf_op jit(solution)/shard_map/pallas_call | solution.py:348

commit v4 on v3

--- a/solution.py
+++ b/solution.py
@@ -69,13 +69,14 @@
             device_id=device, device_id_type=MESH,
         )
 
-    def own_copy(d, target):
-        return remote(kv.at[me], kv.at[me], kv_send.at[d], kv_recv.at[me], peer(target))
-
-    def relay_copy(d, slot):
+    def kv_copy(slot, part, send, device):
         return remote(
-            kv.at[slot], kv.at[slot], kv_send.at[span // 2 + d], kv_recv.at[slot], peer(sibling)
-        )
+            kv.at[slot, part], kv.at[slot, part], kv_send.at[send, part],
+            kv_recv.at[slot, part], device,
+        )
+
+    def own_parts(d):
+        return (0, 1) if d <= 1 else (side,)
 
     def sib_copy(d):
         return remote(
@@ -99,11 +100,13 @@
     for d, target in enumerate(partners, 1):
         @pl.when(target > me)
         def _():
-            own_copy(d, target).start()
+            for part in own_parts(d):
+                kv_copy(me, part, d, peer(target)).start()
 
     @pl.when(sibling > me)
     def _():
-        own_copy(0, sibling).start()
+        for part in (0, 1):
+            kv_copy(me, part, 0, peer(sibling)).start()
 
     for h in range(heads):
         at = slice(h * rows, (h + 1) * rows)
@@ -169,11 +172,32 @@
 
         @pl.when(s < me)
         def _():
-            relay_copy(0, s).wait_recv()
-
-            @pl.when(t % 2 == 0)
+            d = t // 2
+
+            @pl.when(t >= 4)
             def _():
-                relay_copy(t // 2, s).start()
+                @pl.when(t % 2 == 0)
+                def _():
+                    kv_copy(s, side, 0, twin).wait_recv()
+                    kv_copy(s, side, span + d, twin).start()
+                    kv_copy(s, side, span // 2 + d, peer(sibling)).start()
+                    kv_copy(s, 1 - side, 0, twin).wait_recv()
+                    kv_copy(s, 1 - side, span // 2 + d, peer(sibling)).start()
+
+                @pl.when(t % 2 == 1)
+                def _():
+                    for part in (0, 1):
+                        kv_copy(s, part, 0, twin).wait_recv()
+
+            @pl.when(t < 4)
+            def _():
+                for part in (0, 1):
+                    kv_copy(s, part, 0, twin).wait_recv()
+
+                @pl.when(t == 2)
+                def _():
+                    for part in (0, 1):
+                        kv_copy(s, part, span // 2 + d, peer(sibling)).start()
 
             stat_block(s, False)
 
@@ -267,7 +291,8 @@
 
     @pl.when(sibling > me)
     def _():
-        own_copy(0, sibling).wait_send()
+        for part in (0, 1):
+            kv_copy(me, part, 0, peer(sibling)).wait_send()
 
     @pl.when(sibling < me)
     def _():
@@ -276,11 +301,15 @@
     for d, target in enumerate(partners, 1):
         @pl.when(target > me)
         def _():
-            own_copy(d, target).wait_send()
+            for part in own_parts(d):
+                kv_copy(me, part, d, peer(target)).wait_send()
 
         @pl.when(target < me)
         def _():
-            relay_copy(d, target).wait_send()
+            for part in (0, 1):
+                kv_copy(target, part, span // 2 + d, peer(sibling)).wait_send()
+            if d > 1:
+                kv_copy(target, side, span + d, twin).wait_send()
             sib_copy(d).wait_send()
             for part in (0, 1):
                 red_copy(d, part, target).wait_send()
@@ -333,8 +362,8 @@
             pltpu.VMEM((span // 2,) + pair, BF16),
             pltpu.VMEM(pair, BF16),
             pltpu.VMEM(pair, BF16),
-            pltpu.SemaphoreType.DMA((span,)),
-            pltpu.SemaphoreType.DMA((span,)),
+            pltpu.SemaphoreType.DMA((2 * span, 2)),
+            pltpu.SemaphoreType.DMA((span, 2)),
             pltpu.SemaphoreType.DMA((span // 2,)),
             pltpu.SemaphoreType.DMA((span // 2,)),
             pltpu.SemaphoreType.DMA((span // 2, 2)),

time: 45.5 us -> 55.9 us (1.23)
  the two profiles are of different devices: /device:TPU:0 before, /device:TPU:18 now
where the time goes in v4:
time: 55.9 us; the launch traced here: 55.7 us
  Pallas kernels  55.1 us (99%)
  between operations  0.64 us (1%)
    pallas_call x1, Pallas kernels, body(): pl.pallas_call(functools.partial(kernel, span), out_shape=(jax.ShapeDtype...  53.2 us
    pallas_call x1, Pallas kernels, body(): pl.pallas_call(copy_out, out_shape=tuple((jax.ShapeDtypeStruct(g.shape, g...  1.84 us

profile of v4, /device:TPU:18, one launch (start us, length us, event | category | flops | bytes accessed | tf_op | source)
XLA Modules:
  0.0 55.7 jit_solution(5872805141806613842)
XLA Ops:
  0.6 53.2 %shard_map.76 = (bf16[512,256]{1,0:T(8,128)(2,1)}, bf16[512,128]{1,0:T(8,128)(2,1)}, bf16[512,128]{1,0:T(8,128)(2,1)}) custom-call(bf16[512,256]{1,0:T(8,128)(2,1)} %q_ref.1, bf16[512,128]{1,0:T(8,128)(2,1)} %k_ref.1, bf16[512,128]{1,0:T(8,128)(2,1)} %v_ref.1, bf16[512,256]{1,0:T(8,128)(2,1)} %do_ref.1, s32[1,512]{1,0:T(1,128)} %bitcast.1), custom_call_target="tpu_custom_call" | custom-call | tf_op jit(solution)/shard_map/pallas_call | solution.py:331
  53.9 1.8 %shard_map.77 = (bf16[512,256]{1,0:T(8,128)(2,1)}, bf16[512,128]{1,0:T(8,128)(2,1)}, bf16[512,128]{1,0:T(8,128)(2,1)}) custom-call(bf16[512,256]{1,0:T(8,128)(2,1)} %get-tuple-element.6.a, bf16[512,128]{1,0:T(8,128)(2,1)} %get-tuple-element.7.b, bf16[512,128]{1,0:T(8,128)(2,1)} %get-tuple-element.8.c), custom_call_target="tpu_custom_call" | custom-call | tf_op jit(solution)/shard_map/pallas_call | solution.py:377

commit v5 on v3

--- a/solution.py
+++ b/solution.py
@@ -32,9 +32,10 @@
     span,
     q_ref, k_ref, v_ref, do_ref, start_ref,
     dq_ref, dk_ref, dv_ref,
-    kv, qs, dos, qt, dot_t, e_all, d_all, raw0, raw1, p0, p1, ds0, ds1, m_run, l_run, w_run, dq_t, acc,
+    kv, qs, dos, qt, dot_t, e_all, d_all, raw0, raw1, p0, p1, ds0, ds1, m_run, l_run, w_run, dq_t, acc, own,
     sib_out, sib_in, red_out, red_in, hd_out, hd_in,
-    kv_send, kv_recv, sib_send, sib_recv, red_send, red_recv, hd_sem,
+    far_q, far_do, far_stat, stat_out, far_dq, far_dq_out, far_dq_in, mid_out, mid_in,
+    kv_send, kv_recv, sib_send, sib_recv, red_send, red_recv, hd_sem, far_send, far_recv,
 ):
     rows = k_ref.shape[0]
     heads = q_ref.shape[1] // HDIM
@@ -59,9 +60,11 @@
     partners = [xor3(me, 2 * d) for d in range(1, span // 2)]
 
     barrier = pltpu.get_barrier_semaphore()
-    for other in [peer(sibling), twin] + [peer(p, hd) for p in partners for hd in (0, 1)]:
+    greeted = [peer(sibling), twin, peer(partners[2])]
+    greeted += [peer(p, hd) for p in partners[:2] for hd in (0, 1)]
+    for other in greeted:
         pl.semaphore_signal(barrier, inc=1, device_id=other, device_id_type=MESH)
-    pl.semaphore_wait(barrier, 2 + 2 * len(partners))
+    pl.semaphore_wait(barrier, len(greeted))
 
     def remote(src, dst, send, recv, device):
         return pltpu.make_async_remote_copy(
@@ -87,6 +90,17 @@
             red_out.at[d, part], red_in.at[d, side], red_send.at[d, part],
             red_recv.at[d, side], peer(target, part),
         )
+
+    helps, relays, owns = me // 2 == 1, me // 2 == 2, me // 2 == 3
+    across = peer(partners[1])
+
+    def far_copy(i):
+        src, dst = (
+            (qs, far_q), (dos, far_do), (stat_out, far_stat), (far_dq_out, far_dq_in),
+        )[i]
+        return remote(src, dst, far_send.at[i], far_recv.at[i], across)
+
+    mid_copy = remote(mid_out, mid_in, far_send.at[4], far_recv.at[4], peer(partners[0]))
 
     def red_arrival(d, source):
         return remote(
@@ -113,6 +127,12 @@
         dos[at, :] = g
         qt[:, at] = q.T
         dot_t[:, at] = g.T
+
+    @pl.when(owns)
+    def _():
+        far_copy(0).start()
+        far_copy(1).start()
+
     m_run[...] = jnp.full_like(m_run, MASKED)
     l_run[...] = jnp.zeros_like(l_run)
     w_run[...] = jnp.zeros_like(w_run)
@@ -184,31 +204,90 @@
     w_run[...] = w_run[...] / l_run[...]
     m_run[...] = m_run[...] + jnp.log2(l_run[...])
 
+    @pl.when(owns)
+    def _():
+        stat_out[0] = m_run[...]
+        stat_out[1] = w_run[...]
+        for h in range(heads):
+            stat_out[2, :, h * rows:(h + 1) * rows] = start_ref[...].astype(F32)
+        far_copy(2).start()
+
+    def grad_block(slot, s, norm_of, delta_of, q_rows, do_rows, dq_sum, add):
+        dq_term = None
+        for kc in range(rows // chunk):
+            p_low, ds_low = p_halves[kc], ds_halves[kc]
+            for tq in range(wide // tile):
+                at_q = slice(tq * tile, (tq + 1) * tile)
+                norm, delta = norm_of(at_q), delta_of(at_q)
+                for r in range(0, chunk, piece):
+                    at_k = slice(kc * chunk + r, kc * chunk + r + piece)
+                    p = jnp.exp2(e_all[slot, at_k, at_q] - norm)
+                    ds = p * (d_all[slot, at_k, at_q] - delta)
+                    p_low[r:r + piece, at_q] = p.astype(BF16)
+                    ds_low[r:r + piece, at_q] = ds.astype(BF16)
+            at_k = slice(kc * chunk, (kc + 1) * chunk)
+            key_term = dot(ds_low[...], q_rows[...])
+            value_term = dot(p_low[...], do_rows[...])
+            acc[0, at_k, :] = acc[0, at_k, :] + key_term if add else key_term
+            acc[1, at_k, :] = acc[1, at_k, :] + value_term if add else value_term
+            term = dot(kv[s, 0, at_k, :], ds_low[...], ((0,), (0,)))
+            dq_term = term if dq_term is None else dq_term + term
+        dq_sum[...] += dq_term
+
+
+    def far_block(s):
+        slot = s + span // 2
+        first_row = (base + s) * rows
+        key_pos = lax.broadcasted_iota(jnp.int32, (piece, tile), 0).astype(F32)
+        for tq in range(wide // tile):
+            at_q = slice(tq * tile, (tq + 1) * tile)
+            first = far_stat[2, :, at_q] - first_row.astype(F32)
+            raw[tq % 2][...] = dot(kv[s, 0], qt[:, at_q])
+            d_all[slot, :, at_q] = dot(kv[s, 1], dot_t[:, at_q])
+            for r in range(0, rows, piece):
+                at_k = slice(r, r + piece)
+                scores = raw[tq % 2][at_k, :] * scale2
+                e_all[slot, at_k, at_q] = jnp.where(key_pos >= first - r, scores, MASKED)
+        grad_block(
+            slot, s, lambda at: far_stat[0, :, at], lambda at: far_stat[1, :, at],
+            far_q, far_do, far_dq, True,
+        )
+
+    turn = 2 * helps.astype(jnp.int32)
+
     def grad_step(i, _):
-        t = span - 1 - i
+        t = xor3(span - 1 - i, turn)
         s = xor3(me, t)
         d = t // 2
 
-        @pl.when(s <= me)
-        def _():
-            dq_term = None
-            for kc in range(rows // chunk):
-                p_low, ds_low = p_halves[kc], ds_halves[kc]
-                for tq in range(wide // tile):
-                    at_q = slice(tq * tile, (tq + 1) * tile)
-                    norm, delta = m_run[:, at_q], w_run[:, at_q]
-                    for r in range(0, chunk, piece):
-                        at_k = slice(kc * chunk + r, kc * chunk + r + piece)
-                        p = jnp.exp2(e_all[s, at_k, at_q] - norm)
-                        ds = p * (d_all[s, at_k, at_q] - delta)
-                        p_low[r:r + piece, at_q] = p.astype(BF16)
-                        ds_low[r:r + piece, at_q] = ds.astype(BF16)
-                at_k = slice(kc * chunk, (kc + 1) * chunk)
-                acc[0, at_k, :] = dot(ds_low[...], qs[...])
-                acc[1, at_k, :] = dot(p_low[...], dos[...])
-                term = dot(kv[s, 0, at_k, :], ds_low[...], ((0,), (0,)))
-                dq_term = term if dq_term is None else dq_term + term
-            dq_t[...] += dq_term
+        @pl.when((s <= me) & ((t < 6) | (me // 2 != 3)))
+        def _():
+            grad_block(
+                s, s, lambda at: m_run[:, at], lambda at: w_run[:, at], qs, dos, dq_t, False
+            )
+
+            @pl.when(helps & (t == 3))
+            def _():
+                for i in range(3):
+                    far_copy(i).wait_recv()
+                far_dq[...] = jnp.zeros_like(far_dq)
+                for h in range(heads):
+                    at = slice(h * rows, (h + 1) * rows)
+                    qt[:, at] = far_q[at, :].T
+                    dot_t[:, at] = far_do[at, :].T
+
+            @pl.when(helps & (t // 2 == 1))
+            def _():
+                far_block(s)
+
+            @pl.when(helps & (t == 2))
+            def _():
+                far_dq_out[...] = far_dq[...].astype(BF16)
+                far_copy(3).start()
+
+            @pl.when(t == 0)
+            def _():
+                own[...] = acc[...]
 
             @pl.when(t % 2 == 1)
             def _():
@@ -218,7 +297,21 @@
             @pl.when((t % 2 == 0) & (t > 0))
             def _():
                 sib_copy(d).wait_recv()
-                red_out[d] = (acc[...] + sib_in[d].astype(F32)).astype(BF16)
+                acc[...] += sib_in[d].astype(F32)
+
+            @pl.when(owns & (t == 4))
+            def _():
+                mid_copy.wait_recv()
+                acc[...] += mid_in[...].astype(F32)
+
+            @pl.when(t == 6)
+            def _():
+                mid_out[...] = acc[...].astype(BF16)
+                mid_copy.start()
+
+            @pl.when((t % 2 == 0) & (t > 0) & (t < 6))
+            def _():
+                red_out[d] = acc[...].astype(BF16)
                 for part in (0, 1):
                     red_copy(d, part, s).start()
 
@@ -229,11 +322,16 @@
     @pl.when(sibling > me)
     def _():
         sib_copy(0).wait_recv()
-        acc[...] += sib_in[0].astype(F32)
-
-    hd_out[0] = acc[1 - side].astype(BF16)
+        own[...] += sib_in[0].astype(F32)
+
+    hd_out[0] = own[1 - side].astype(BF16)
     swap = remote(hd_out.at[0], hd_in.at[0], hd_sem.at[0], hd_sem.at[1], twin)
     swap.start()
+
+    @pl.when(owns)
+    def _():
+        far_copy(3).wait_recv()
+        dq_t[...] += far_dq_in[...].astype(F32)
 
     for h in range(heads):
         dq_ref[:, h * HDIM:(h + 1) * HDIM] = (
@@ -241,16 +339,16 @@
         )
 
     swap.wait()
-    acc[side] += hd_in[0].astype(F32)
-
-    for d, target in enumerate(partners, 1):
+    own[side] += hd_in[0].astype(F32)
+
+    for d, target in enumerate(partners[:2], 1):
         @pl.when(target > me)
         def _():
             for source in (0, 1):
                 red_arrival(d, source).wait_recv()
-                acc[side] += red_in[d, source].astype(F32)
-
-    hd_out[1] = (acc[side] * jnp.where(side == 0, scaling, 1.0)).astype(BF16)
+                own[side] += red_in[d, source].astype(F32)
+
+    hd_out[1] = (own[side] * jnp.where(side == 0, scaling, 1.0)).astype(BF16)
     finished = remote(hd_out.at[1], hd_in.at[1], hd_sem.at[2], hd_sem.at[3], twin)
     finished.start()
     finished.wait()
@@ -281,9 +379,24 @@
         @pl.when(target < me)
         def _():
             relay_copy(d, target).wait_send()
-            sib_copy(d).wait_send()
-            for part in (0, 1):
-                red_copy(d, part, target).wait_send()
+            if d < 3:
+                sib_copy(d).wait_send()
+                for part in (0, 1):
+                    red_copy(d, part, target).wait_send()
+
+    @pl.when(relays)
+    def _():
+        sib_copy(3).wait_send()
+        mid_copy.wait_send()
+
+    @pl.when(owns)
+    def _():
+        for i in range(3):
+            far_copy(i).wait_send()
+
+    @pl.when(helps)
+    def _():
+        far_copy(3).wait_send()
 
 
 def copy_out(a, b, c, out_a, out_b, out_c):
@@ -327,10 +440,20 @@
             pltpu.VMEM((1, wide), F32),
             pltpu.VMEM((HDIM, wide), F32),
             pltpu.VMEM(pair, F32),
+            pltpu.VMEM(pair, F32),
             pltpu.VMEM((span // 2,) + pair, BF16),
             pltpu.VMEM((span // 2,) + pair, BF16),
             pltpu.VMEM((span // 2,) + pair, BF16),
             pltpu.VMEM((span // 2,) + pair, BF16),
+            pltpu.VMEM(pair, BF16),
+            pltpu.VMEM(pair, BF16),
+            pltpu.VMEM((wide, HDIM), BF16),
+            pltpu.VMEM((wide, HDIM), BF16),
+            pltpu.VMEM((3, 1, wide), F32),
+            pltpu.VMEM((3, 1, wide), F32),
+            pltpu.VMEM((HDIM, wide), F32),
+            pltpu.VMEM((HDIM, wide), BF16),
+            pltpu.VMEM((HDIM, wide), BF16),
             pltpu.VMEM(pair, BF16),
             pltpu.VMEM(pair, BF16),
             pltpu.SemaphoreType.DMA((span,)),
@@ -340,6 +463,8 @@
             pltpu.SemaphoreType.DMA((span // 2, 2)),
             pltpu.SemaphoreType.DMA((span // 2, 2)),
             pltpu.SemaphoreType.DMA((4,)),
+            pltpu.SemaphoreType.DMA((5,)),
+            pltpu.SemaphoreType.DMA((5,)),
         ],
         compiler_params=pltpu.CompilerParams(
             collective_id=0, has_side_effects=True, vmem_limit_bytes=56 * 1024 * 1024

time: 45.5 us -> 48.5 us (1.066)
  the two profiles are of different devices: /device:TPU:0 before, /device:TPU:8 now
where the time goes in v5:
time: 48.5 us; the launch traced here: 48.4 us
  Pallas kernels  47.7 us (98%)
  between operations  0.64 us (1%)
    pallas_call x1, Pallas kernels, body(): pl.pallas_call(functools.partial(kernel, span), out_shape=(jax.ShapeDtype...  45.9 us
    pallas_call x1, Pallas kernels, body(): pl.pallas_call(copy_out, out_shape=tuple((jax.ShapeDtypeStruct(g.shape, g...  1.84 us

profile of v5, /device:TPU:8, one launch (start us, length us, event | category | flops | bytes accessed | tf_op | source)
XLA Modules:
  0.0 48.4 jit_solution(13545070716806759859)
XLA Ops:
  0.6 45.9 %shard_map.76 = (bf16[512,256]{1,0:T(8,128)(2,1)}, bf16[512,128]{1,0:T(8,128)(2,1)}, bf16[512,128]{1,0:T(8,128)(2,1)}) custom-call(bf16[512,256]{1,0:T(8,128)(2,1)} %q_ref.1, bf16[512,128]{1,0:T(8,128)(2,1)} %k_ref.1, bf16[512,128]{1,0:T(8,128)(2,1)} %v_ref.1, bf16[512,256]{1,0:T(8,128)(2,1)} %do_ref.1, s32[1,512]{1,0:T(1,128)} %bitcast.1), custom_call_target="tpu_custom_call" | custom-call | tf_op jit(solution)/shard_map/pallas_call | solution.py:415
  46.5 1.8 %shard_map.77 = (bf16[512,256]{1,0:T(8,128)(2,1)}, bf16[512,128]{1,0:T(8,128)(2,1)}, bf16[512,128]{1,0:T(8,128)(2,1)}) custom-call(bf16[512,256]{1,0:T(8,128)(2,1)} %get-tuple-element.6.a, bf16[512,128]{1,0:T(8,128)(2,1)} %get-tuple-element.7.b, bf16[512,128]{1,0:T(8,128)(2,1)} %get-tuple-element.8.c), custom_call_target="tpu_custom_call" | custom-call | tf_op jit(solution)/shard_map/pallas_call | solution.py:473

commit v6 on v5

--- a/solution.py
+++ b/solution.py
@@ -34,7 +34,7 @@
     dq_ref, dk_ref, dv_ref,
     kv, qs, dos, qt, dot_t, e_all, d_all, raw0, raw1, p0, p1, ds0, ds1, m_run, l_run, w_run, dq_t, acc, own,
     sib_out, sib_in, red_out, red_in, hd_out, hd_in,
-    far_q, far_do, far_stat, stat_out, far_dq, far_dq_out, far_dq_in, mid_out, mid_in,
+    far_q, far_do, far_stat, stat_out, far_start, start_out, far_dq, far_dq_out, far_dq_in, mid_out, mid_in,
     kv_send, kv_recv, sib_send, sib_recv, red_send, red_recv, hd_sem, far_send, far_recv,
 ):
     rows = k_ref.shape[0]
@@ -97,10 +97,11 @@
     def far_copy(i):
         src, dst = (
             (qs, far_q), (dos, far_do), (stat_out, far_stat), (far_dq_out, far_dq_in),
+            (start_out, far_start),
         )[i]
         return remote(src, dst, far_send.at[i], far_recv.at[i], across)
 
-    mid_copy = remote(mid_out, mid_in, far_send.at[4], far_recv.at[4], peer(partners[0]))
+    mid_copy = remote(mid_out, mid_in, far_send.at[5], far_recv.at[5], peer(partners[0]))
 
     def red_arrival(d, source):
         return remote(
@@ -130,8 +131,11 @@
 
     @pl.when(owns)
     def _():
+        for h in range(heads):
+            start_out[:, h * rows:(h + 1) * rows] = start_ref[...].astype(F32)
         far_copy(0).start()
         far_copy(1).start()
+        far_copy(4).start()
 
     m_run[...] = jnp.full_like(m_run, MASKED)
     l_run[...] = jnp.zeros_like(l_run)
@@ -208,8 +212,6 @@
     def _():
         stat_out[0] = m_run[...]
         stat_out[1] = w_run[...]
-        for h in range(heads):
-            stat_out[2, :, h * rows:(h + 1) * rows] = start_ref[...].astype(F32)
         far_copy(2).start()
 
     def grad_block(slot, s, norm_of, delta_of, q_rows, do_rows, dq_sum, add):
@@ -235,30 +237,34 @@
         dq_sum[...] += dq_term
 
 
-    def far_block(s):
+    def far_scores(s):
         slot = s + span // 2
         first_row = (base + s) * rows
         key_pos = lax.broadcasted_iota(jnp.int32, (piece, tile), 0).astype(F32)
         for tq in range(wide // tile):
             at_q = slice(tq * tile, (tq + 1) * tile)
-            first = far_stat[2, :, at_q] - first_row.astype(F32)
+            first = far_start[:, at_q] - first_row.astype(F32)
             raw[tq % 2][...] = dot(kv[s, 0], qt[:, at_q])
             d_all[slot, :, at_q] = dot(kv[s, 1], dot_t[:, at_q])
             for r in range(0, rows, piece):
                 at_k = slice(r, r + piece)
                 scores = raw[tq % 2][at_k, :] * scale2
                 e_all[slot, at_k, at_q] = jnp.where(key_pos >= first - r, scores, MASKED)
+
+    def far_block(s):
         grad_block(
-            slot, s, lambda at: far_stat[0, :, at], lambda at: far_stat[1, :, at],
+            s + span // 2, s, lambda at: far_stat[0, :, at], lambda at: far_stat[1, :, at],
             far_q, far_do, far_dq, True,
         )
 
-    turn = 2 * helps.astype(jnp.int32)
+    helping, owning = helps.astype(jnp.int32), owns.astype(jnp.int32)
 
     def grad_step(i, _):
-        t = xor3(span - 1 - i, turn)
+        pair = i // 2
+        d = 3 - pair + owning * (((pair + 1) // 2) % 2) * (2 * pair - 3)
+        d = d + helping * (1 - 2 * (d % 2))
+        t = 2 * d + 1 - i % 2
         s = xor3(me, t)
-        d = t // 2
 
         @pl.when((s <= me) & ((t < 6) | (me // 2 != 3)))
         def _():
@@ -268,13 +274,16 @@
 
             @pl.when(helps & (t == 3))
             def _():
-                for i in range(3):
+                for i in (0, 1, 4):
                     far_copy(i).wait_recv()
                 far_dq[...] = jnp.zeros_like(far_dq)
                 for h in range(heads):
                     at = slice(h * rows, (h + 1) * rows)
                     qt[:, at] = far_q[at, :].T
                     dot_t[:, at] = far_do[at, :].T
+                far_scores(s)
+                far_scores(xor3(me, 2))
+                far_copy(2).wait_recv()
 
             @pl.when(helps & (t // 2 == 1))
             def _():
@@ -391,7 +400,7 @@
 
     @pl.when(owns)
     def _():
-        for i in range(3):
+        for i in (0, 1, 2, 4):
             far_copy(i).wait_send()
 
     @pl.when(helps)
@@ -449,8 +458,10 @@
             pltpu.VMEM(pair, BF16),
             pltpu.VMEM((wide, HDIM), BF16),
             pltpu.VMEM((wide, HDIM), BF16),
-            pltpu.VMEM((3, 1, wide), F32),
-            pltpu.VMEM((3, 1, wide), F32),
+            pltpu.VMEM((2, 1, wide), F32),
+            pltpu.VMEM((2, 1, wide), F32),
+            pltpu.VMEM((1, wide), F32),
+            pltpu.VMEM((1, wide), F32),
             pltpu.VMEM((HDIM, wide), F32),
             pltpu.VMEM((HDIM, wide), BF16),
             pltpu.VMEM((HDIM, wide), BF16),
@@ -463,8 +474,8 @@
             pltpu.SemaphoreType.DMA((span // 2, 2)),
             pltpu.SemaphoreType.DMA((span // 2, 2)),
             pltpu.SemaphoreType.DMA((4,)),
-            pltpu.SemaphoreType.DMA((5,)),
-            pltpu.SemaphoreType.DMA((5,)),
+            pltpu.SemaphoreType.DMA((6,)),
+            pltpu.SemaphoreType.DMA((6,)),
         ],
         compiler_params=pltpu.CompilerParams(
             collective_id=0, has_side_effects=True, vmem_limit_bytes=56 * 1024 * 1024

time: 48.5 us -> 45.1 us (0.930)
  the two profiles are of different devices: /device:TPU:8 before, /device:TPU:0 now
where the time goes in v6:
time: 45.1 us; the launch traced here: 44.3 us
  Pallas kernels  43.7 us (97%)
  between operations  0.64 us (1%)
    pallas_call x1, Pallas kernels, body(): pl.pallas_call(functools.partial(kernel, span), out_shape=(jax.ShapeDtype...  41.8 us
    pallas_call x1, Pallas kernels, body(): pl.pallas_call(copy_out, out_shape=tuple((jax.ShapeDtypeStruct(g.shape, g...  1.84 us

profile of v6, /device:TPU:0, one launch (start us, length us, event | category | flops | bytes accessed | tf_op | source)
XLA Modules:
  0.0 44.3 jit_solution(16486966356991844241)
XLA Ops:
  0.6 41.8 %shard_map.76 = (bf16[512,256]{1,0:T(8,128)(2,1)}, bf16[512,128]{1,0:T(8,128)(2,1)}, bf16[512,128]{1,0:T(8,128)(2,1)}) custom-call(bf16[512,256]{1,0:T(8,128)(2,1)} %q_ref.1, bf16[512,128]{1,0:T(8,128)(2,1)} %k_ref.1, bf16[512,128]{1,0:T(8,128)(2,1)} %v_ref.1, bf16[512,256]{1,0:T(8,128)(2,1)} %do_ref.1, s32[1,512]{1,0:T(1,128)} %bitcast.1), custom_call_target="tpu_custom_call" | custom-call | tf_op jit(solution)/shard_map/pallas_call | solution.py:424
  42.5 1.8 %shard_map.77 = (bf16[512,256]{1,0:T(8,128)(2,1)}, bf16[512,128]{1,0:T(8,128)(2,1)}, bf16[512,128]{1,0:T(8,128)(2,1)}) custom-call(bf16[512,256]{1,0:T(8,128)(2,1)} %get-tuple-element.6.a, bf16[512,128]{1,0:T(8,128)(2,1)} %get-tuple-element.7.b, bf16[512,128]{1,0:T(8,128)(2,1)} %get-tuple-element.8.c), custom_call_target="tpu_custom_call" | custom-call | tf_op jit(solution)/shard_map/pallas_call | solution.py:484

commit v7 on v6

--- a/solution.py
+++ b/solution.py
@@ -111,7 +111,7 @@
 
     kv[me, 0] = k_ref[...]
     kv[me, 1] = v_ref[...]
-    for d, target in enumerate(partners, 1):
+    for d, target in reversed(list(enumerate(partners, 1))):
         @pl.when(target > me)
         def _():
             own_copy(d, target).start()
@@ -321,7 +321,7 @@
             @pl.when((t % 2 == 0) & (t > 0) & (t < 6))
             def _():
                 red_out[d] = acc[...].astype(BF16)
-                for part in (0, 1):
+                for part in (1 - side, side):
                     red_copy(d, part, s).start()
 
         return 0

time: 45.1 us -> 46.8 us (1.038)
  Pallas kernels: 43.7 us -> 45.5 us
    pallas_call x1, Pallas kernels: 41.8 us -> 43.7 us  [body(): pl.pallas_call(functools.partial(kernel, span), out_shape=(jax.ShapeDtype...]
where the time goes in v7:
time: 46.8 us; the launch traced here: 46.2 us
  Pallas kernels  45.5 us (97%)
  between operations  0.64 us (1%)
    pallas_call x1, Pallas kernels, body(): pl.pallas_call(functools.partial(kernel, span), out_shape=(jax.ShapeDtype...  43.7 us
    pallas_call x1, Pallas kernels, body(): pl.pallas_call(copy_out, out_shape=tuple((jax.ShapeDtypeStruct(g.shape, g...  1.84 us

profile of v7, /device:TPU:0, one launch (start us, length us, event | category | flops | bytes accessed | tf_op | source)
XLA Modules:
  0.0 46.2 jit_solution(12171495922081431521)
XLA Ops:
  0.6 43.7 %shard_map.76 = (bf16[512,256]{1,0:T(8,128)(2,1)}, bf16[512,128]{1,0:T(8,128)(2,1)}, bf16[512,128]{1,0:T(8,128)(2,1)}) custom-call(bf16[512,256]{1,0:T(8,128)(2,1)} %q_ref.1, bf16[512,128]{1,0:T(8,128)(2,1)} %k_ref.1, bf16[512,128]{1,0:T(8,128)(2,1)} %v_ref.1, bf16[512,256]{1,0:T(8,128)(2,1)} %do_ref.1, s32[1,512]{1,0:T(1,128)} %bitcast.1), custom_call_target="tpu_custom_call" | custom-call | tf_op jit(solution)/shard_map/pallas_call | solution.py:424
  44.3 1.8 %shard_map.77 = (bf16[512,256]{1,0:T(8,128)(2,1)}, bf16[512,128]{1,0:T(8,128)(2,1)}, bf16[512,128]{1,0:T(8,128)(2,1)}) custom-call(bf16[512,256]{1,0:T(8,128)(2,1)} %get-tuple-element.6.a, bf16[512,128]{1,0:T(8,128)(2,1)} %get-tuple-element.7.b, bf16[512,128]{1,0:T(8,128)(2,1)} %get-tuple-element.8.c), custom_call_target="tpu_custom_call" | custom-call | tf_op jit(solution)/shard_map/pallas_call | solution.py:484
